TPU v7x, 256 devices: a whole 4x4x8 slice. The times are simulated.
256 devices in a mesh: vel: 16 (over z, core), space: 16 (over x, y).
Axes of the slice: x: 4, y: 4, z: 8, core: 2. Of those that a mesh axis runs over, the one named last changes fastest.
Arguments:
- particle_distribution: float32 [2048, 32, 2048], P('vel', None, 'space'), may hold values from 0 to 7, as said below
- piece_warmth: float32 [256], P('space'), may hold values from 0.6 to 1.8
- exterior_piece_label: int32 [2048], P('space'), may hold values from -1 to 255, as said below
Outputs:
- following_distribution: float32 [2048, 32, 2048], P('vel', None, 'space')
- revised_piece_warmth: float32 [256], P('space')
Inputs may be any that keep to these rules, and one draw needn't show every extreme that they name: `particle_distribution`: every entry is positive. `exterior_piece_label`: one cyclic run of 512 consecutive columns holds the solid elements 0 to 255 in order, each on 2 consecutive columns; all other columns hold -1.
All inputs are finite; a program needn't handle non-finite values.
Results may differ from a plain program's by a relative error of at most 0.0003.
Values sent between devices are 32-bit elements; how exact they have to be, the bound alone decides.
A program may use at most 64 MiB of HBM per device.

v0:
```python
import math

import jax
import jax.numpy as jnp
from jax import lax
from jax.sharding import PartitionSpec as P

STEP_DURATION = 0.25
HALF_STEP = 0.125
COLLISION_SPAN = 8.0
WEIGHT = 0.25
TUBE_TRANSFER = 0.45
CONDUCTION_LINK = 0.1
CEILING_TIER = lax.Precision.HIGHEST


def padded(cells, sides, width, closed):
    for axis, dim in sides:
        count = lax.axis_size(axis)
        ends = count if closed else count - 1
        head = lax.slice_in_dim(cells, 0, width, axis=dim)
        tail = lax.slice_in_dim(cells, cells.shape[dim] - width, cells.shape[dim], axis=dim)
        cells = jnp.concatenate(
            [
                lax.ppermute(tail, axis, [(i, (i + 1) % count) for i in range(ends)]),
                cells,
                lax.ppermute(head, axis, [((i + 1) % count, i) for i in range(ends)]),
            ],
            axis=dim,
        )
    return cells


def speeds(offset, number):
    indices = offset + jnp.arange(number, dtype=jnp.int32)
    lengthwise_position = ((indices // 128).astype(jnp.float32) - 7.5) * 0.5
    circumferential_bearing = (indices // 16 % 8).astype(jnp.float32) - 3.5
    spanwise_position = ((indices % 16).astype(jnp.float32) - 7.5) * 0.5
    return (lengthwise_position, spanwise_position, circumferential_bearing)


def moment_table(lengthwise_position, spanwise_position, circumferential_bearing):
    internal_enthalpy = 0.5 * (
        lengthwise_position * lengthwise_position
        + spanwise_position * spanwise_position
        + circumferential_bearing * circumferential_bearing
    )
    return WEIGHT * jnp.stack(
        [
            jnp.ones_like(lengthwise_position),
            lengthwise_position,
            spanwise_position,
            circumferential_bearing,
            internal_enthalpy,
        ]
    )


def wall_table(lengthwise_position, spanwise_position, circumferential_bearing):
    internal_enthalpy = 0.5 * (
        lengthwise_position * lengthwise_position
        + spanwise_position * spanwise_position
        + circumferential_bearing * circumferential_bearing
    )
    upward = spanwise_position > 0.0
    inward = jnp.where(upward, spanwise_position, 0.0)
    outward = jnp.where(upward, 0.0, -spanwise_position)
    return WEIGHT * jnp.stack(
        [inward, inward * internal_enthalpy, outward, outward * internal_enthalpy]
    )


def moments(moment_rows, values):
    flattened = values.reshape(values.shape[0], -1)
    summed = jnp.dot(moment_rows, flattened, precision=CEILING_TIER)
    return summed.reshape((moment_rows.shape[0],) + values.shape[1:])


def gas_state(quadrature_totals):
    particle_concentration = quadrature_totals[0]
    lengthwise_speed = quadrature_totals[1] / particle_concentration
    spanwise_speed = quadrature_totals[2] / particle_concentration
    circumferential_speed = quadrature_totals[3] / particle_concentration
    fluid_warmth = (
        2.0 * quadrature_totals[4] / particle_concentration
        - (
            lengthwise_speed * lengthwise_speed
            + spanwise_speed * spanwise_speed
            + circumferential_speed * circumferential_speed
        )
    ) / 3.0
    collision_frequency = (
        COLLISION_SPAN * jnp.exp(-0.19 * jnp.log(fluid_warmth)) / particle_concentration
    )
    return jnp.stack(
        [
            particle_concentration,
            lengthwise_speed,
            spanwise_speed,
            circumferential_speed,
            fluid_warmth,
            collision_frequency,
        ]
    )


def maxwell(lengthwise_position, spanwise_position, circumferential_bearing, hydrodynamic_fields):
    warmth_spread = (
        (lengthwise_position - hydrodynamic_fields[1]) ** 2
        + (spanwise_position - hydrodynamic_fields[2]) ** 2
        + (circumferential_bearing - hydrodynamic_fields[3]) ** 2
    )
    return hydrodynamic_fields[0] * jnp.exp(
        -1.5 * jnp.log(2.0 * math.pi * hydrodynamic_fields[4])
        - warmth_spread / (2.0 * hydrodynamic_fields[4])
    )


def half_step(
    values, hydrodynamic_fields, lengthwise_position, spanwise_position, circumferential_bearing
):
    doubled = 2.0 * hydrodynamic_fields[5]
    target = maxwell(
        lengthwise_position, spanwise_position, circumferential_bearing, hydrodynamic_fields
    )
    return (doubled - HALF_STEP) / (doubled + STEP_DURATION) * values + 3.0 * HALF_STEP / (
        doubled + STEP_DURATION
    ) * target


def face_mix(
    values, hydrodynamic_fields, lengthwise_position, spanwise_position, circumferential_bearing
):
    doubled = 2.0 * hydrodynamic_fields[5]
    target = maxwell(
        lengthwise_position, spanwise_position, circumferential_bearing, hydrodynamic_fields
    )
    return doubled / (doubled + HALF_STEP) * values + HALF_STEP / (doubled + HALF_STEP) * target


def minmod(forward, backward):
    return (
        0.5
        * (jnp.sign(forward) + jnp.sign(backward))
        * jnp.minimum(jnp.abs(forward), jnp.abs(backward))
    )


def upwind_faces(widened, velocity, dimension):
    number = widened.shape[dimension] - 4
    steps_along = lax.slice_in_dim(widened, 1, number + 4, axis=dimension) - lax.slice_in_dim(
        widened, 0, number + 3, axis=dimension
    )
    slopes = minmod(
        lax.slice_in_dim(steps_along, 1, number + 3, axis=dimension),
        lax.slice_in_dim(steps_along, 0, number + 2, axis=dimension),
    )
    upper = lax.slice_in_dim(widened, 1, number + 2, axis=dimension) + (
        0.5 - velocity * HALF_STEP
    ) * lax.slice_in_dim(slopes, 0, number + 1, axis=dimension)
    lower = lax.slice_in_dim(widened, 2, number + 3, axis=dimension) + (
        -0.5 - velocity * HALF_STEP
    ) * lax.slice_in_dim(slopes, 1, number + 2, axis=dimension)
    return jnp.where(velocity > 0.0, upper, lower)


def mirror(values):
    number = values.shape[0]
    folded = values.reshape((number // 16, 16) + values.shape[1:])
    return jnp.flip(folded, 1).reshape(values.shape)


def with_ghosts(values):
    flipped = mirror(values)
    return jnp.concatenate(
        [flipped[:, 1:2], flipped[:, 0:1], values, flipped[:, -1:], flipped[:, -2:-1]], axis=1
    )


def boundary_maxwellian_field(
    lengthwise_position, spanwise_position, circumferential_bearing, interface_warmth
):
    internal_enthalpy = 0.5 * (
        lengthwise_position * lengthwise_position
        + spanwise_position * spanwise_position
        + circumferential_bearing * circumferential_bearing
    )
    return jnp.exp(
        -1.5 * jnp.log(2.0 * math.pi * interface_warmth) - internal_enthalpy / interface_warmth
    )


def wall_heat(wall_sums, strip_touches_tube):
    wall_density = wall_sums[0] / wall_sums[2]
    return jnp.where(strip_touches_tube, wall_sums[1] - wall_density * wall_sums[3], 0.0)


def wall_faces(
    flux_radial, outer_values, wall_sums, boundary_maxwellian, strip_touches_tube, radial_column
):
    wall_density = wall_sums[0] / wall_sums[2]
    reflected = jnp.where(radial_column > 0.0, outer_values, wall_density * boundary_maxwellian)
    outer_face = jnp.where(strip_touches_tube, reflected, flux_radial[:, -1])
    return jnp.concatenate([flux_radial[:, :-1], outer_face[:, None]], axis=1)


def advance(values, plus_half, flux_axial, flux_radial, lengthwise_position, spanwise_position):
    return (
        4.0 / 3.0 * plus_half
        - values / 3.0
        - STEP_DURATION
        * (
            lengthwise_position * (flux_axial[:, :, 1:] - flux_axial[:, :, :-1])
            + spanwise_position * (flux_radial[:, 1:] - flux_radial[:, :-1])
        )
    )


def cell_state(partial_value):
    return gas_state(lax.psum(partial_value, "vel"))


def per_device(particle_distribution, piece_warmth, exterior_piece_label):
    number, radial_cells, columns = particle_distribution.shape
    lengthwise_position, spanwise_position, circumferential_bearing = speeds(
        lax.axis_index("vel") * number, number
    )
    axial_grid = lengthwise_position[:, None, None]
    radial_grid = spanwise_position[:, None, None]
    azimuth_grid = circumferential_bearing[:, None, None]
    moment_rows = moment_table(lengthwise_position, spanwise_position, circumferential_bearing)
    macro_cells = cell_state(moments(moment_rows, particle_distribution))
    plus_local = half_step(
        particle_distribution, macro_cells, axial_grid, radial_grid, azimuth_grid
    )
    widened = padded(plus_local, (("space", 2),), 2, True)
    plus_half = widened[:, :, 2:-2]
    values_axial = upwind_faces(widened, axial_grid, 2)
    values_radial = upwind_faces(with_ghosts(plus_half), radial_grid, 1)
    warmth_reservoir = lax.all_gather(piece_warmth, "space", axis=0, tiled=True)
    piece_label = jnp.arange(warmth_reservoir.shape[0], dtype=jnp.int32)
    piece_marker = (exterior_piece_label[None, :] == piece_label[:, None]).astype(jnp.float32)
    strip_touches_tube = exterior_piece_label >= 0
    interface_warmth = jnp.where(
        strip_touches_tube, jnp.dot(warmth_reservoir, piece_marker, precision=CEILING_TIER), 1.0
    )
    boundary_maxwellian = boundary_maxwellian_field(
        lengthwise_position[:, None],
        spanwise_position[:, None],
        circumferential_bearing[:, None],
        interface_warmth,
    )
    outer_values = values_radial[:, -1]
    wall_weights = wall_table(lengthwise_position, spanwise_position, circumferential_bearing)
    wall_part = jnp.concatenate(
        [
            jnp.dot(wall_weights[0:2], outer_values, precision=CEILING_TIER),
            jnp.dot(wall_weights[2:4], boundary_maxwellian, precision=CEILING_TIER),
        ]
    )
    sums_axial = moments(moment_rows, values_axial)
    sums_radial = moments(moment_rows, values_radial)
    total_axial, total_radial, wall_sums = lax.psum((sums_axial, sums_radial, wall_part), "vel")
    macro_axial = gas_state(total_axial)
    macro_radial = gas_state(total_radial)
    heat_flow = wall_heat(wall_sums, strip_touches_tube)
    flux_axial = face_mix(values_axial, macro_axial, axial_grid, radial_grid, azimuth_grid)
    flux_radial = face_mix(values_radial, macro_radial, axial_grid, radial_grid, azimuth_grid)
    flux_radial = wall_faces(
        flux_radial,
        outer_values,
        wall_sums,
        boundary_maxwellian,
        strip_touches_tube,
        spanwise_position[:, None],
    )
    following_distribution = advance(
        particle_distribution, plus_half, flux_axial, flux_radial, axial_grid, radial_grid
    )
    local_strip_total = piece_warmth.shape[0]
    owned_ids = lax.axis_index("space") * local_strip_total + jnp.arange(
        local_strip_total, dtype=jnp.int32
    )
    heat_terms = lax.all_gather(heat_flow, "space", axis=0, tiled=True)
    owners = lax.all_gather(exterior_piece_label, "space", axis=0, tiled=True)
    chosen = (owners[None, :] == owned_ids[:, None]).astype(jnp.float32)
    warmth_received = jnp.dot(chosen, heat_terms, precision=CEILING_TIER)
    condition_spread = piece_warmth - 1.0
    ghost_margin = padded(condition_spread, (("space", 0),), 1, False)
    revised_piece_warmth = (
        piece_warmth
        + TUBE_TRANSFER * (ghost_margin[:-2] - 2.0 * condition_spread + ghost_margin[2:])
        + CONDUCTION_LINK * STEP_DURATION * warmth_received
    )
    return (following_distribution, revised_piece_warmth)


def solution(mesh):
    return jax.shard_map(
        per_device,
        mesh=mesh,
        in_specs=(P("vel", None, "space"), P("space"), P("space")),
        out_specs=(P("vel", None, "space"), P("space")),
        check_vma=False,
    )
```

profile of v0, /device:TPU:1, one launch (start us, length us, event | category | flops | bytes accessed | tf_op | source)
XLA Modules:
  0.0 357.0 jit_solution(1575963030795156224)
XLA Ops:
  7.3 4.5 %copy.54 = f32[16,8,32,128]{3,1,2,0:T(8,128)} copy(f32[16,8,32,128]{3,2,1,0:T(8,128)} %bitcast.113) | data formatting | bytes 4194304
  11.8 1.9 copy.24
  13.8 1.8 fusion.42
  17.0 4.6 %collective-permute-start.2 = (f32[1]{0:T(128)}, f32[1]{0:T(128)}, u32[]{:S(2)}, u32[]{:S(2)}) collective-permute-start(f32[1]{0:T(128)} %get-tuple-element.43), channel_id=1, source_target_pairs={{0,1},{1,2},{2,3},{3,4},{4,5},{5,6},{6,7},{7,8},{8,9},{9,10},{10,1... | collective-permute-start | bytes 20 | tf_op jit(solution)/shard_map/ppermute | solution.py:25
  24.5 34.2 %all-reduce = f32[256]{0:T(256)S(1)} all-reduce(f32[256]{0:T(256)S(1)} %dynamic-update-slice), channel_id=1, replica_groups=mesh['vel'=16,'space'=16] {'space'}, use_global_device_ids=true, to_apply=%add | all-reduce | flops 256 | bytes 2048
  58.8 13.0 %all-gather = s32[16,1,128]{2,1,0:T(1,128)S(1)} all-gather(s32[1,1,128]{2,1,0:T(1,128)S(1)} %bitcast.129), channel_id=1, replica_groups=mesh['vel'=16,'space'=16] {'space'}, dimensions={0}, use_global_device_ids=true | all-gather | bytes 8704 | tf_op jit(solution)/shard_map/all_gather | solution.py:285
  73.4 48.3 %all-reduce.5.cloned.1.call-done = f32[5,32,128]{2,1,0:T(8,128)} async-done(((f32[5,32,128]{2,1,0:T(8,128)}), f32[5,32,128]{2,1,0:T(8,128)}) %all-reduce.5.cloned.1.call-update) | async-done | bytes 81936 | tf_op jit(solution)/shard_map/psum | solution.py:220
  123.3 2.6 multiply_add_fusion.2
  125.9 2.8 fusion.84
  130.2 1.8 fusion.85
  132.8 1.9 minimum_multiply_fusion.1
  134.7 2.4 fusion.4
  137.0 3.3 copy.34
  141.4 2.7 copy.26
  145.5 2.7 copy.28
  148.1 3.6 %collective-permute-start.1 = (f32[128,32,2]{0,1,2:T(8,128)S(1)}, f32[128,32,2]{0,1,2:T(8,128)S(1)}, u32[]{:S(2)}, u32[]{:S(2)}) collective-permute-start(f32[128,32,2]{0,1,2:T(8,128)S(1)} %copy.28), channel_id=1, source_target_pairs={{1,0},{2,1},{3,2},{4,3},{5,4},{6,5},{7,6},{8,7},{9,8},{10,9},{11,1... | collective-permute-start | bytes 98312 | tf_op jit(solution)/shard_map/ppermute | solution.py:27
  151.7 4.2 %fusion.6 = f32[5,33,128]{2,0,1:T(8,128)} fusion(f32[128,33,128]{0,2,1:T(8,128)} %copy.34, f32[5,128]{1,0:T(8,128)S(1)} %stack.4), kind=kOutput, calls=%fused_computation.19 | convolution fusion | flops 32440960 | bytes 2249728 | tf_op jit(solution)/shard_map/dot_general | solution.py:75
  156.1 23.8 %psum.31 = f32[4,128]{1,0:T(4,128)S(1)} all-reduce(f32[4,128]{1,0:T(4,128)S(1)} %pad_maximum_fusion.4), channel_id=1, replica_groups=mesh['vel'=16,'space'=16] {'vel'}, use_global_device_ids=true, to_apply=%region_3.4 | all-reduce | flops 512 | bytes 4096 | tf_op jit(solution)/shard_map/psum | solution.py:263
  179.9 14.6 %all-gather.1 = f32[16,1,128]{2,1,0:T(1,128)S(1)} all-gather(f32[1,1,128]{2,1,0:T(1,128)S(1)} %get-tuple-element.6), channel_id=1, replica_groups=mesh['vel'=16,'space'=16] {'space'}, dimensions={0}, use_global_device_ids=true | all-gather | bytes 8704 | tf_op jit(solution)/shard_map/all_gather | solution.py:284
  194.5 2.9 copy.27
  197.4 2.9 copy.30
  200.2 3.9 %pad_maximum_fusion.2 = f32[128,32,132]{2,1,0:T(8,128)S(1)} fusion(f32[128,32,2]{2,1,0:T(8,128)} %copy.30, f32[128,32,128]{2,1,0:T(8,128)S(1)} %multiply_add_fusion.2, f32[128,32,2]{2,1,0:T(8,128)} %copy.27), kind=kLoop, calls=%fused_computation.8 | loop fusion | flops 1081344 | bytes 4325376 | tf_op jit(solution)/shard_map/concatenate | solution.py:23
  205.4 2.9 minimum_multiply_fusion
  208.3 5.2 %fusion.1 = f32[128,32,129]{2,1,0:T(8,128)} fusion(f32[128,32,130]{2,1,0:T(8,128)S(1)} %minimum_multiply_fusion, f32[128,32,2]{2,1,0:T(8,128)S(1)} %copy-done.4, f32[128,32,128]{2,1,0:T(8,128)S(1)} %multiply_add_fusion.2, f32[128,32,2]{2,1,0:T(8,128)S(1)} %copy-done.3, f32[128]{0:T(128)S(1)} %get-tuple-element.57, f32[128]{0:T(128)S(1)} %get-tuple-element.58, ...), kind=kLoop, calls=%fused_computation.2 | loop fusion | flops 3698688 | bytes 8504448 | tf_op jit(solution)/shard_map/jit(_where)/select_n | solution.py:164
  213.5 3.9 %reshape.518 = f32[128,4128]{1,0:T(8,128)S(1)} reshape(f32[128,32,129]{2,1,0:T(8,128)} %fusion.1) | data formatting | bytes 4227072 | tf_op jit(solution)/shard_map/reshape | solution.py:74
  217.4 1.9 copy.35
  219.3 2.7 dot_general.37
  222.1 5.3 %fusion.40 = f32[5,32,129]{2,0,1:T(8,128)S(1)} fusion(f32[32,129,128]{2,1,0:T(8,128)} %dot_general.37, f32[5,128]{1,0:T(8,128)S(1)} %stack.4), kind=kOutput, calls=%fused_computation.100 | convolution fusion | flops 31703680 | bytes 2198656 | tf_op jit(solution)/shard_map/dot_general | solution.py:75
  228.9 108.0 %all-reduce.7.cloned.1.call-done = (f32[5,33,128]{2,0,1:T(8,128)}, f32[5,32,129]{2,1,0:T(8,128)}) async-done(((f32[5,33,128]{2,0,1:T(8,128)}, f32[5,32,129]{2,1,0:T(8,128)}), (f32[5,33,128]{2,0,1:T(8,128)}, f32[5,32,129]{2,1,0:T(8,128)})) %all-reduce.7.cloned.1.call-update) | async-done | bytes 167056 | tf_op jit(solution)/shard_map/psum | solution.py:263
  340.3 1.6 multiply_add_fusion.1
  344.1 2.6 multiply_add_fusion
  346.7 3.4 fusion.12
  (77 shorter events, 20.2 us)
Async XLA Ops:
  7.2 114.5 %all-reduce.5.cloned.1.call-start = ((), (), s32[]{:S(2)}) async-start(), calls=%async_computation | async-start | bytes 163840 | tf_op jit(solution)/shard_map/psum | solution.py:220
  11.8 4.6 %copy-start.6 = (f32[16]{0:T(128)S(1)}, f32[16]{0:T(128)}, u32[]{:S(2)}) copy-start(f32[16]{0:T(128)} %param.4) | copy-start | bytes 196
  11.8 11.2 %copy-start.7 = (u32[256]{0:T(256)S(1)}, u32[256]{0:T(256)}, u32[]{:S(2)}) copy-start(u32[256]{0:T(256)} %constant.159) | copy-start | bytes 3076
  11.8 46.9 %copy-start.5 = (s32[128]{0:T(128)S(1)}, s32[128]{0:T(128)}, u32[]{:S(2)}) copy-start(s32[128]{0:T(128)} %param.5) | copy-start | bytes 1540
  16.3 320.6 %all-reduce.7.cloned.1.call-start = ((), (), s32[]{:S(2)}) async-start(), calls=%async_computation.1 | async-start | bytes 598016 | tf_op jit(solution)/shard_map/psum | solution.py:263
  17.0 55.1 %collective-permute-start.2 = (f32[1]{0:T(128)}, f32[1]{0:T(128)}, u32[]{:S(2)}, u32[]{:S(2)}) collective-permute-start(f32[1]{0:T(128)} %get-tuple-element.43), channel_id=1, source_target_pairs={{0,1},{1,2},{2,3},{3,4},{4,5},{5,6},{6,7},{7,8},{8,9},{9,10},{10,1... | collective-permute-start | bytes 20 | tf_op jit(solution)/shard_map/ppermute | solution.py:25
  21.5 50.6 %collective-permute-start.3 = (f32[1]{0:T(128)}, f32[1]{0:T(128)}, u32[]{:S(2)}, u32[]{:S(2)}) collective-permute-start(f32[1]{0:T(128)} %get-tuple-element.44), channel_id=1, source_target_pairs={{1,0},{2,1},{3,2},{4,3},{5,4},{6,5},{7,6},{8,7},{9,8},{10,9},{11,1... | collective-permute-start | bytes 20 | tf_op jit(solution)/shard_map/ppermute | solution.py:27
  144.0 50.5 %collective-permute-start = (f32[128,32,2]{0,1,2:T(8,128)S(1)}, f32[128,32,2]{0,1,2:T(8,128)S(1)}, u32[]{:S(2)}, u32[]{:S(2)}) collective-permute-start(f32[128,32,2]{0,1,2:T(8,128)S(1)} %copy.26), channel_id=1, source_target_pairs={{0,1},{1,2},{2,3},{3,4},{4,5},{5,6},{6,7},{7,8},{8,9},{9,10},{10,1... | collective-permute-start | bytes 98312 | tf_op jit(solution)/shard_map/ppermute | solution.py:25
  148.1 49.2 %collective-permute-start.1 = (f32[128,32,2]{0,1,2:T(8,128)S(1)}, f32[128,32,2]{0,1,2:T(8,128)S(1)}, u32[]{:S(2)}, u32[]{:S(2)}) collective-permute-start(f32[128,32,2]{0,1,2:T(8,128)S(1)} %copy.28), channel_id=1, source_target_pairs={{1,0},{2,1},{3,2},{4,3},{5,4},{6,5},{7,6},{8,7},{9,8},{10,9},{11,1... | collective-permute-start | bytes 98312 | tf_op jit(solution)/shard_map/ppermute | solution.py:27
  205.4 2.9 copy-start.3
  205.4 2.9 copy-start.4
  222.1 118.2 %copy-start.1 = (f32[128,33,128]{2,1,0:T(8,128)S(1)}, f32[128,33,128]{2,1,0:T(8,128)}, u32[]{:S(2)}) copy-start(f32[128,33,128]{2,1,0:T(8,128)} %fusion.4) | copy-start | bytes 6488068
  341.9 2.2 copy-start
  344.1 2.6 copy-start.2
Sparse Core Ops, SparseCore 0:
  16.4 105.2 all-reduce.4
  228.3 108.6 all-reduce.6
where the time goes:
time: 358 us; the launch traced here: 357 us
  waiting for transfers between devices  156 us (44%)
  blocking collectives  85.6 us (24%)
  local copies, waits for them, and re-layouts  41.2 us (12%)
  other arithmetic  35.1 us (10%)
  between operations  15 us (4%)
  matrix products  12.6 us (4%)
  starting transfers between devices  11 us (3%)
    psum x1, waiting for transfers between devices, per_device(): lax.psum((sums_axial, sums_radial, wall_part), 'vel')  108 us
    psum x1, waiting for transfers between devices, cell_state(): return gas_state(lax.psum(partial_value, 'vel'))  48.3 us
    unnamed x1, blocking collectives  34.2 us
    psum x1, blocking collectives, per_device(): lax.psum((sums_axial, sums_radial, wall_part), 'vel')  23.8 us
    all_gather x1, blocking collectives, per_device(): heat_terms = lax.all_gather(heat_flow, 'space', axis=0, tiled=True)  14.6 us
    all_gather x1, blocking collectives, per_device(): owners = lax.all_gather(exterior_piece_label, 'space', axis=0, tiled=True)  13 us
    dot_general x3, matrix products, moments(): summed = jnp.dot(moment_rows, flattened, precision=CEILING_TIER)  11.3 us
    select_n x2, other arithmetic, upwind_faces(): return jnp.where(velocity > 0.0, upper, lower)  7.56 us
  transfers between devices with their start and end apart: 6, of which 2 were waited for; matrix products, arithmetic and copies ran while one was open for 4% of the time, Pallas kernels for 0%

commit v1 on v0

v1 whole, which is shorter than its diff:
```python
import functools
import math

import jax
import jax.numpy as jnp
from jax import lax
from jax.experimental import pallas as pl
from jax.experimental.pallas import tpu as pltpu
from jax.sharding import PartitionSpec as P

MESH = pl.DeviceIdType.MESH
N = 16
ROWS = 32
LANES = 128
TWO_PI = 2.0 * math.pi
BITREV = (0, 4, 2, 6, 1, 5, 3, 7)
F32 = jnp.float32


def iota(axis):
    return lax.broadcasted_iota(jnp.int32, (8, LANES), axis)


def spread(row):
    return jnp.broadcast_to(row, (8, LANES))


def minmod(p, q):
    return jnp.maximum(jnp.minimum(p, 0.0), jnp.minimum(jnp.maximum(p, 0.0), q))


def flip8(x, sub):
    x = pltpu.roll(x, 4, 0)
    x = jnp.where((sub & 2) == 0, pltpu.roll(x, 6, 0), pltpu.roll(x, 2, 0))
    return jnp.where((sub & 1) == 0, pltpu.roll(x, 7, 0), pltpu.roll(x, 1, 0))


def merge(a, b, h, sub):
    low = (sub & h) == 0
    if h == 4:
        return jnp.where(low, a, b) + pltpu.roll(jnp.where(low, b, a), 4, 0)
    return jnp.where(low, a, pltpu.roll(b, h, 0)) + jnp.where(
        low, pltpu.roll(a, 8 - h, 0), b
    )


def stack_sums(parts, sub):
    x = [parts[BITREV[i]] for i in range(8)]
    x = [merge(x[2 * i], x[2 * i + 1], 4, sub) for i in range(4)]
    x = [merge(x[2 * i], x[2 * i + 1], 2, sub) for i in range(2)]
    return merge(x[0], x[1], 1, sub)


def z_sums(v):
    s = [v[4 + j] + v[3 - j] for j in range(4)]
    d = [v[4 + j] - v[3 - j] for j in range(4)]
    total = (s[0] + s[1]) + (s[2] + s[3])
    first = (0.5 * d[0] + 1.5 * d[1]) + (2.5 * d[2] + 3.5 * d[3])
    second = (0.25 * s[0] + 2.25 * s[1]) + (6.25 * s[2] + 12.25 * s[3])
    return total, first, second


def quads(low, high, y):
    s0, z0, zz0 = z_sums(low)
    s1, z1, zz1 = z_sums(high)
    a0, a1 = y[0] * s0, y[1] * s1
    return (s0 + s1, a0 + a1, z0 + z1, (y[0] * a0 + y[1] * a1) + (zz0 + zz1)), (
        a1,
        y[1] * (y[1] * a1 + zz1),
    )


def gas(total, by_x, by_xx, sub, face):
    s0 = total
    ux = by_x / s0
    uy = pltpu.roll(total, 6, 0) / s0
    uz = pltpu.roll(total, 4, 0) / s0
    rho = 0.25 * s0
    temp = ((by_xx + pltpu.roll(total, 2, 0)) / s0 - (ux * ux + uy * uy + uz * uz)) / 3.0
    tau = 8.0 * jnp.exp(-0.19 * jnp.log(temp)) / rho
    if face:
        mix = 2.0 * tau / (2.0 * tau + 0.125)
        share = 0.125 / (2.0 * tau + 0.125)
    else:
        mix = (2.0 * tau - 0.125) / (2.0 * tau + 0.25)
        share = 0.375 / (2.0 * tau + 0.25)
    weight = share * rho * jnp.exp(-1.5 * jnp.log(TWO_PI * temp))
    half = 0.5 / temp
    first = jnp.where(
        sub < 2,
        mix,
        jnp.where(
            sub < 4,
            pltpu.roll(weight, 2, 0),
            jnp.where(sub < 6, pltpu.roll(ux, 4, 0), pltpu.roll(uy, 6, 0)),
        ),
    )
    second = jnp.where(sub < 2, uz, pltpu.roll(half, 2, 0))
    return first, second


def gather_sums(ref):
    total = by_x = by_xx = None
    for k in range(N):
        x = 0.5 * (k - 7.5)
        t = ref[k]
        if k == 0:
            total, by_x, by_xx = t, x * t, (x * x) * t
        else:
            total, by_x, by_xx = total + t, by_x + x * t, by_xx + (x * x) * t
    return total, by_x, by_xx


def kernel(
    f_hbm, pw_ref, lab_ref, out_hbm, rev_ref,
    fv, plus, gx, gy,
    s1, r1, a1, sx, rx, ax_f, sy, ry, ay_f, s32, r32, sex, rex,
    warm, heat, pk, pku, pkd, cpk, gpk, prev, x8_ref, fx_ref, fp_ref,
    in_sem, out_sem, send, recv, hsend, hrecv,
):
    me = lax.axis_index("vel")
    sp = lax.axis_index("space")
    ip = (me >= 8).astype(jnp.int32)
    dirn = 2 * ip - 1
    xi_x = 0.5 * (me.astype(F32) - 7.5)
    abs_x = xi_x * dirn.astype(F32)
    sub, lane = iota(0), iota(1)
    subf = sub.astype(F32)
    y = (0.5 * (subf - 7.5), 0.5 * (subf + 0.5))
    zed = subf - 3.5
    step_dn = lax.rem(dirn + 128, 128)
    step_up = lax.rem(128 - dirn, 128)
    at_up = lane == 127 - 127 * ip
    at_dn = lane == 127 * ip
    is_pos = lane < 128 * ip

    def vel_copy(group, d, src, dst):
        peer = lax.rem(me + d, N)
        return pltpu.make_async_remote_copy(
            src, dst, send.at[group, d], recv.at[group, d],
            device_id={"vel": peer}, device_id_type=MESH,
        )

    def space_copy(group, d, src, dst):
        peer = lax.rem(sp + d, N)
        return pltpu.make_async_remote_copy(
            src, dst, hsend.at[group, d], hrecv.at[group, d],
            device_id={"space": peer}, device_id_type=MESH,
        )

    def wait_all(copier, group, buf, mine, ready=True):
        @pl.loop(1, N)
        def _(d):
            src = lax.rem(mine - d + N, N)
            c = copier(group, d, buf.at[src], buf.at[src])
            if ready:
                c.wait_recv()
            else:
                c.wait_send()

    @pl.loop(0, ROWS)
    def _(r):
        pltpu.make_async_copy(f_hbm.at[:, r], fv.at[r], in_sem.at[r]).start()

    barrier = pltpu.get_barrier_semaphore()

    @pl.loop(1, N)
    def _(d):
        pl.semaphore_signal(
            barrier, 1, device_id={"vel": lax.rem(me + d, N)}, device_id_type=MESH
        )
        pl.semaphore_signal(
            barrier, 1, device_id={"space": lax.rem(sp + d, N)}, device_id_type=MESH
        )

    own = jnp.broadcast_to(pw_ref[...], (16, 16))
    diag = lax.broadcasted_iota(jnp.int32, (16, 16), 0) == lax.broadcasted_iota(
        jnp.int32, (16, 16), 1
    )
    own = jnp.sum(jnp.where(diag, own, 0.0), axis=1, keepdims=True)
    warm[sp] = jnp.broadcast_to(own, (16, LANES))
    zero = jnp.zeros((8, LANES), F32)
    for i in range(16):
        pk[i] = zero

    def load16(ref, r):
        return [
            [ref[r, pl.ds(iz * 16 + half * 8, 8), :] for iz in range(8)] for half in range(2)
        ]

    @pl.loop(0, N)
    def _(o):
        parts = [None] * 8
        for row in range(2):
            r = 2 * o + row
            pltpu.make_async_copy(f_hbm.at[:, r], fv.at[r], in_sem.at[r]).wait()
            v = load16(fv, r)
            q, _w = quads(v[0], v[1], y)
            for i in range(4):
                parts[2 * i + row] = q[i]
        s1[o] = stack_sums(parts, sub)

    r1[me] = s1[me]
    pl.semaphore_wait(barrier, 2 * (N - 1))

    @pl.loop(1, N)
    def _(d):
        peer = lax.rem(me + d, N)
        vel_copy(0, d, s1.at[peer], r1.at[me]).start()

    @pl.loop(1, N)
    def _(d):
        space_copy(0, d, warm.at[sp], warm.at[sp]).start()

    wait_all(vel_copy, 0, r1, me)
    first, second = gas(*gather_sums(r1), sub, False)
    a1[me, 0:8, :] = first
    a1[me, 8:16, :] = second

    @pl.loop(1, N)
    def _(d):
        vel_copy(1, d, a1.at[me], a1.at[me]).start()

    wait_all(space_copy, 0, warm, sp)
    label = spread(lab_ref[...])
    walled = label >= 0
    tw_sum = zero
    for k in range(N):
        for h in range(2):
            tw_sum = tw_sum + jnp.where(
                label == k * 16 + h * 8 + sub, warm[k, pl.ds(8 * h, 8), :], 0.0
            )
    tw_sum = spread(jnp.sum(tw_sum, axis=0, keepdims=True))
    tw = jnp.where(walled, tw_sum, 1.0)
    half_tw = 0.5 / tw
    wall_norm = jnp.exp(-1.5 * jnp.log(TWO_PI * tw))
    e_xy = jnp.exp(-(y[1] * y[1]) * half_tw)
    e_z = jnp.exp(-(zed * zed) * half_tw)

    def down(t):
        return spread(jnp.sum(t, axis=0, keepdims=True))

    sum_x, sum_xx = 2.0 * down(e_xy), 2.0 * down(y[1] * y[1] * e_xy)
    sum_z, sum_zz = down(e_z), down(zed * zed * e_z)
    sum_y1, sum_y3 = down(y[1] * e_xy), down(y[1] * y[1] * y[1] * e_xy)
    out_mass = wall_norm * (sum_x * sum_z * sum_y1)
    out_energy = 0.5 * wall_norm * (
        sum_xx * sum_z * sum_y1 + sum_x * sum_zz * sum_y1 + sum_x * sum_z * sum_y3
    )

    wait_all(vel_copy, 1, a1, me)

    def factors(first, second, row):
        mix = spread(first[0 + row : 1 + row])
        weight = spread(first[2 + row : 3 + row])
        ux = spread(first[4 + row : 5 + row])
        uy = spread(first[6 + row : 7 + row])
        uz = spread(second[0 + row : 1 + row])
        half = spread(second[2 + row : 3 + row])
        ey = [jnp.exp(-((y[h] - uy) * (y[h] - uy)) * half) for h in range(2)]
        dz, dx = zed - uz, xi_x - ux
        bz = weight * jnp.exp(-(dz * dz + dx * dx) * half)
        return mix, ey, bz

    @pl.loop(0, N)
    def _(o):
        first, second = a1[o, 0:8, :], a1[o, 8:16, :]
        for row in range(2):
            r = 2 * o + row
            mix, ey, bz = factors(first, second, row)
            shift = 4 * r + 1 + ip
            mask = (lane >= 4 * r) & (lane <= 4 * r + 2)
            for iz in range(8):
                b = spread(bz[iz : iz + 1])
                for h in range(2):
                    at = pl.ds(iz * 16 + h * 8, 8)
                    p = mix * fv[r, at, :] + ey[h] * b
                    plus[r + 2, at, :] = p
                    i = iz * 2 + h
                    pk[i] = jnp.where(mask, pltpu.roll(p, shift, 1), pk[i])

    down_d = lax.rem(dirn + N, N)
    up_d = lax.rem(N - dirn, N)
    to_down = pltpu.make_async_remote_copy(
        pk, pku, hsend.at[2, 0], hrecv.at[2, 0],
        device_id={"space": lax.rem(sp + down_d, N)}, device_id_type=MESH,
    )
    to_up = pltpu.make_async_remote_copy(
        pk, pkd, hsend.at[2, 1], hrecv.at[2, 1],
        device_id={"space": lax.rem(sp + up_d, N)}, device_id_type=MESH,
    )
    to_down.start()
    to_up.start()

    for ghost, real in ((1, 2), (0, 3), (34, 33), (35, 32)):
        @pl.loop(0, 8)
        def _(iz):
            lo = pl.multiple_of(iz * 16, 8)
            hi = pl.multiple_of(iz * 16 + 8, 8)
            x0, x1 = plus[real, pl.ds(lo, 8), :], plus[real, pl.ds(hi, 8), :]
            plus[ghost, pl.ds(lo, 8), :] = flip8(x1, sub)
            plus[ghost, pl.ds(hi, 8), :] = flip8(x0, sub)

    cy = (0.5 + 0.125 * y[0], 0.5 - 0.125 * y[1])

    def y_face(j):
        v = [[None] * 8, [None] * 8]
        for iz in range(8):
            for h in range(2):
                at = pl.ds(iz * 16 + h * 8, 8)
                if h:
                    c, b, a = plus[j + 1, at, :], plus[j, at, :], plus[j + 2, at, :]
                else:
                    c, b, a = plus[j + 2, at, :], plus[j + 3, at, :], plus[j + 1, at, :]
                g = c + cy[h] * minmod(a - c, c - b)
                gy[j, at, :] = g
                v[h][iz] = g
        return quads(v[0], v[1], y)

    def ship(group, o, src, dst_own, dst):
        d = lax.rem(o - me + N, N)

        @pl.when(d != 0)
        def _():
            vel_copy(group, d, src.at[o], dst.at[me]).start()

    q, w = y_face(32)
    s32[...] = stack_sums([q[0], w[0], q[1], w[1], q[2], zero, q[3], zero], sub)
    r32[me] = s32[...]

    @pl.loop(1, N)
    def _(d):
        vel_copy(2, d, s32, r32.at[me]).start()

    @pl.loop(0, N)
    def _(i):
        o = lax.rem(me + 8 + i, N)
        parts = [None] * 8
        for row in range(2):
            q, _w = y_face(2 * o + row)
            for k in range(4):
                parts[2 * k + row] = q[k]
        sy[o] = stack_sums(parts, sub)
        ship(3, o, sy, None, ry)

    ry[me] = sy[me]

    to_down.wait_recv()
    to_up.wait_recv()
    cx = 0.5 - 0.125 * abs_x
    centre = (lane & 3) == 1
    v = [[None] * 8, [None] * 8]
    for iz in range(8):
        for h in range(2):
            i = iz * 2 + h
            u = pku[i]
            own_pk = pk[i]
            u2 = pltpu.roll(u, step_dn, 1)
            w0 = pltpu.roll(own_pk, step_up, 1)
            d_o = pltpu.roll(pkd[i], step_up, 1)
            g = u + cx * minmod(w0 - u, u - u2)
            gpk[i] = g
            v[h][iz] = g
            cpk[i] = jnp.where(centre, u, pltpu.roll(d_o - own_pk, step_up, 1))
    q, _w = quads(v[0], v[1], y)
    parts = [None] * 8
    for k in range(4):
        parts[2 * k] = q[k]
        parts[2 * k + 1] = pltpu.roll(q[k], 124, 1)
    x8 = stack_sums(parts, sub)
    x8_ref[...] = x8
    sex[...] = jnp.where(is_pos, 0.0, x8)

    @pl.loop(0, N)
    def _(i):
        o = lax.rem(me + 8 + i, N)
        parts = [None] * 8
        for row in range(2):
            r = 2 * o + row
            shift = 126 - 4 * r + ip
            v = [[None] * 8, [None] * 8]
            for iz in range(8):
                for h in range(2):
                    at = pl.ds(iz * 16 + h * 8, 8)
                    p = plus[r + 2, at, :]
                    edge = pltpu.roll(cpk[iz * 2 + h], shift, 1)
                    e = p - jnp.where(at_up, edge, pltpu.roll(p, step_dn, 1))
                    en = jnp.where(at_dn, edge, pltpu.roll(e, step_up, 1))
                    g = p + cx * minmod(en, e)
                    gx[r, at, :] = g
                    v[h][iz] = g
            q, _w = quads(v[0], v[1], y)
            for k in range(4):
                parts[2 * k + row] = q[k]
        t = stack_sums(parts, sub)
        at_o = (lane == 8 * o + 1) & is_pos
        sex[...] = jnp.where(at_o, pltpu.roll(t, 8 * o + 2, 1), sex[...])
        sx[o] = jnp.where(
            lane < ip, pltpu.roll(x8_ref[...], 127 - 8 * o, 1), pltpu.roll(t, ip, 1)
        )
        ship(4, o, sx, None, rx)

    rx[me] = sx[me]
    rex[me] = sex[...]

    @pl.loop(1, N)
    def _(d):
        vel_copy(5, d, sex, rex.at[me]).start()

    @pl.loop(0, ROWS)
    def _(r):
        for i in range(16):
            at = pl.ds(i * 8, 8)
            fv[r, at, :] = (4.0 / 3.0) * plus[r + 2, at, :] - fv[r, at, :] * (1.0 / 3.0)

    wait_all(vel_copy, 3, ry, me)
    first, second = gas(*gather_sums(ry), sub, True)
    ay_f[me, 0:8, :] = first
    ay_f[me, 8:16, :] = second

    @pl.loop(1, N)
    def _(d):
        vel_copy(6, d, ay_f.at[me], ay_f.at[me]).start()

    wait_all(vel_copy, 4, rx, me)
    first, second = gas(*gather_sums(rx), sub, True)
    ax_f[me, 0:8, :] = first
    ax_f[me, 8:16, :] = second

    @pl.loop(1, N)
    def _(d):
        vel_copy(7, d, ax_f.at[me], ax_f.at[me]).start()

    wait_all(vel_copy, 2, r32, me)
    total, by_x, by_xx = gather_sums(r32)
    wall_first, wall_second = gas(total, by_x, by_xx, sub, True)
    in_mass = spread(total[1:2])
    in_energy = 0.5 * spread(by_xx[1:2] + total[3:4])
    rho_w = in_mass / out_mass
    flow = jnp.where(walled, 0.25 * (in_energy - rho_w * out_energy), 0.0)
    heat[sp] = jnp.where(sub == 0, flow, label.astype(F32))

    @pl.loop(1, N)
    def _(d):
        space_copy(1, d, heat.at[sp], heat.at[sp]).start()

    wait_all(vel_copy, 5, rex, me)
    fx_first, fx_second = gas(*gather_sums(rex), sub, True)
    fx_ref[0:8, :] = fx_first
    fx_ref[8:16, :] = fx_second

    wait_all(vel_copy, 6, ay_f, me)
    quarter_y = (0.25 * y[0], 0.25 * y[1])

    def y_flux(first, second, row, j):
        mix, ey, bz = factors(first, second, row)
        mix2 = [mix * quarter_y[h] for h in range(2)]
        ey2 = [ey[h] * quarter_y[h] for h in range(2)]
        out = []
        for iz in range(8):
            b = spread(bz[iz : iz + 1])
            for h in range(2):
                at = pl.ds(iz * 16 + h * 8, 8)
                out.append(mix2[h] * gy[j, at, :] + ey2[h] * b)
        return out

    def y_update(r, flux):
        for i in range(16):
            at = pl.ds(i * 8, 8)
            fv[r, at, :] = fv[r, at, :] - (flux[i] - prev[i])
            prev[i] = flux[i]

    flux = y_flux(ay_f[0, 0:8, :], ay_f[0, 8:16, :], 0, 0)
    for i in range(16):
        prev[i] = flux[i]

    @pl.loop(0, N - 1)
    def _(o):
        y_update(2 * o, y_flux(ay_f[o, 0:8, :], ay_f[o, 8:16, :], 1, 2 * o + 1))
        y_update(
            2 * o + 1, y_flux(ay_f[o + 1, 0:8, :], ay_f[o + 1, 8:16, :], 0, 2 * o + 2)
        )

    y_update(30, y_flux(ay_f[N - 1, 0:8, :], ay_f[N - 1, 8:16, :], 1, 31))
    flux = y_flux(wall_first, wall_second, 0, 32)
    ey_w = jnp.exp(-(y[0] * y[0]) * half_tw) * quarter_y[0]
    bz_w = rho_w * wall_norm * jnp.exp(-(zed * zed + xi_x * xi_x) * half_tw)
    for iz in range(8):
        b = spread(bz_w[iz : iz + 1])
        flux[2 * iz] = jnp.where(walled, ey_w * b, flux[2 * iz])
        flux[2 * iz + 1] = jnp.where(
            walled, quarter_y[1] * gy[32, pl.ds(iz * 16 + 8, 8), :], flux[2 * iz + 1]
        )
    y_update(31, flux)

    wait_all(vel_copy, 7, ax_f, me)
    for t in range(2):
        fp_ref[pl.ds(8 * t, 8), :] = jnp.where(is_pos, 0.0, fx_ref[pl.ds(8 * t, 8), :])

    @pl.loop(0, N)
    def _(o):
        at_o = (lane == 8 * o + 1) & is_pos
        for t in range(2):
            rows = pl.ds(8 * t, 8)
            fp_ref[rows, :] = jnp.where(
                at_o, pltpu.roll(ax_f[o, rows, :], 8 * o + 1, 1), fp_ref[rows, :]
            )

    quarter_x = 0.25 * abs_x
    fp = (fp_ref[0:8, :], fp_ref[8:16, :])
    even = (lane & 7) == 1

    def packed(t, i):
        return jnp.where(even, spread(fp[t][i : i + 1]), pltpu.roll(spread(fp[t][i + 1 : i + 2]), 4, 1))

    mix, weight, ux, uy = [packed(0, 2 * i) for i in range(4)]
    uz, half = packed(1, 0), packed(1, 2)
    ey = [jnp.exp(-((y[h] - uy) * (y[h] - uy)) * half) for h in range(2)]
    dx = xi_x - ux
    for iz in range(8):
        dz = (iz - 3.5) - uz
        b = quarter_x * weight * jnp.exp(-(dz * dz + dx * dx) * half)
        for h in range(2):
            i = iz * 2 + h
            gpk[i] = (quarter_x * mix) * gpk[i] + ey[h] * b

    @pl.loop(0, N)
    def _(o):
        field = []
        for t in range(2):
            rows = pl.ds(8 * t, 8)
            field.append(
                jnp.where(
                    (lane == 127) & is_pos,
                    pltpu.roll(fx_ref[rows, :], 126 - 8 * o, 1),
                    pltpu.roll(ax_f[o, rows, :], lax.rem(128 - ip, 128), 1),
                )
            )
        for row in range(2):
            r = 2 * o + row
            shift = 126 - 4 * r + ip
            mix, ey, bz = factors(field[0], field[1], row)
            mix = quarter_x * mix
            bz = quarter_x * bz
            for iz in range(8):
                b = spread(bz[iz : iz + 1])
                for h in range(2):
                    at = pl.ds(iz * 16 + h * 8, 8)
                    flux = mix * gx[r, at, :] + ey[h] * b
                    edge = pltpu.roll(gpk[iz * 2 + h], shift, 1)
                    before = jnp.where(at_up, edge, pltpu.roll(flux, step_dn, 1))
                    gx[r, at, :] = fv[r, at, :] - (flux - before)
            pltpu.make_async_copy(gx.at[r], out_hbm.at[:, r], out_sem.at[r]).start()

    wait_all(space_copy, 1, heat, sp)
    piece = lax.broadcasted_iota(jnp.int32, (16, LANES), 0) + sp * 16
    piecef = piece.astype(F32)
    gained = jnp.zeros((16, LANES), F32)
    for k in range(N):
        t = heat[k]
        gained = gained + jnp.where(
            jnp.broadcast_to(t[1:2], (16, LANES)) == piecef,
            jnp.broadcast_to(t[0:1], (16, LANES)),
            0.0,
        )
    gained = jnp.sum(gained, axis=1, keepdims=True)
    own = warm[sp]
    dev = own - 1.0
    before = jnp.where(sp == 0, 0.0, 1.0) * (warm[lax.rem(sp + N - 1, N), 15:16, :] - 1.0)
    after = jnp.where(sp == N - 1, 0.0, 1.0) * (warm[lax.rem(sp + 1, N), 0:1, :] - 1.0)
    dev_before = jnp.concatenate([before, dev[:-1]], axis=0)
    dev_after = jnp.concatenate([dev[1:], after], axis=0)
    new = own + 0.45 * (dev_before - 2.0 * dev + dev_after) + 0.025 * gained
    on_diag = lax.broadcasted_iota(jnp.int32, (16, LANES), 1) == lax.broadcasted_iota(
        jnp.int32, (16, LANES), 0
    )
    row = jnp.sum(jnp.where(on_diag, new, 0.0), axis=0, keepdims=True)
    rev_ref[...] = row[:, :16]

    to_down.wait_send()
    to_up.wait_send()
    for group, buf in enumerate((r1, a1, r32, ry, rx, rex, ay_f, ax_f)):
        wait_all(vel_copy, group, buf, me, ready=False)
    for group, buf in enumerate((warm, heat)):
        wait_all(space_copy, group, buf, sp, ready=False)

    @pl.loop(0, ROWS)
    def _(r):
        pltpu.make_async_copy(gx.at[r], out_hbm.at[:, r], out_sem.at[r]).wait()


def per_device(particle_distribution, piece_warmth, exterior_piece_label):
    tile = functools.partial(pltpu.VMEM, dtype=F32)
    dma = pltpu.SemaphoreType.DMA
    any_spec = pl.BlockSpec(memory_space=pl.ANY)
    vmem_spec = pl.BlockSpec(memory_space=pltpu.VMEM)
    one = tile((N, 8, LANES))
    two = tile((N, 16, LANES))
    out, revised = pl.pallas_call(
        kernel,
        out_shape=(
            jax.ShapeDtypeStruct(particle_distribution.shape, F32),
            jax.ShapeDtypeStruct((1, 16), F32),
        ),
        in_specs=[any_spec, vmem_spec, vmem_spec],
        out_specs=(any_spec, vmem_spec),
        scratch_shapes=[
            tile((ROWS, 128, LANES)), tile((ROWS + 4, 128, LANES)),
            tile((ROWS, 128, LANES)), tile((ROWS + 1, 128, LANES)),
            one, one, two,
            one, one, two,
            one, one, two,
            tile((8, LANES)), one,
            tile((8, LANES)), one,
            two, one,
            one, one, one, one, one, one,
            tile((8, LANES)), tile((16, LANES)), tile((16, LANES)),
            dma((ROWS,)), dma((ROWS,)),
            dma((8, N)), dma((8, N)), dma((3, N)), dma((3, N)),
        ],
        compiler_params=pltpu.CompilerParams(
            collective_id=0, has_side_effects=True, vmem_limit_bytes=24 * 1024 * 1024
        ),
    )(
        particle_distribution,
        piece_warmth.reshape(1, 16),
        exterior_piece_label.reshape(1, LANES),
    )
    return out, revised.reshape(16)


def solution(mesh):
    return jax.shard_map(
        per_device,
        mesh=mesh,
        in_specs=(P("vel", None, "space"), P("space"), P("space")),
        out_specs=(P("vel", None, "space"), P("space")),
        check_vma=False,
    )
```

time: 358 us -> 65.4 us (0.18)
  waiting for transfers between devices: 156 us -> 0 us
  blocking collectives: 85.6 us -> 0 us
  Pallas kernels: 0 us -> 59.9 us
  local copies, waits for them, and re-layouts: 41.2 us -> 4.73 us
  other arithmetic: 35.1 us -> 0 us
  between operations: 15 us -> 0.65 us
  matrix products: 12.6 us -> 0 us
  starting transfers between devices: 11 us -> 0 us
    psum x2 -> x0, waiting for transfers between devices: 156 us -> none  [the longest x1 108 us: per_device(): lax.psum((sums_axial, sums_radial, wall_part), 'vel')]
    pallas_call x0 -> x1, Pallas kernels: none -> 59.9 us  [per_device(): pl.pallas_call(kernel, out_shape=(jax.ShapeDtypeStruct(particle_distribut...]
    unnamed x1 -> x0, blocking collectives: 34.2 us -> none
    all_gather x2 -> x0, blocking collectives: 27.6 us -> none  [the longest x1 14.6 us: per_device(): heat_terms = lax.all_gather(heat_flow, 'space', axis=0, tiled=True)]
    psum x1 -> x0, blocking collectives: 23.8 us -> none  [per_device(): lax.psum((sums_axial, sums_radial, wall_part), 'vel')]
    dot_general x7 -> x0, matrix products: 12.6 us -> none  [the longest x3 11.3 us: moments(): summed = jnp.dot(moment_rows, flattened, precision=CEILING_TIER)]
    slice x7 -> x0, local copies, waits for them, and re-layouts: 11.8 us -> none  [the longest x3 6.07 us: padded(): lax.slice_in_dim(cells, cells.shape[dim] - width, cells.shape[dim], axis=...]
    ppermute x4 -> x0, starting transfers between devices: 10.9 us -> none  [the longest x2 6 us: padded(): lax.ppermute(tail, axis, [(i, (i + 1) % count) for i in range(ends)])]
  transfers between devices with their start and end apart: 6 -> 0, of which waited for: 2 -> 0; matrix products, arithmetic and copies ran while one was open for 4% -> 0% of each run, Pallas kernels for 0% -> 0%
where the time goes in v1:
time: 65.4 us; the launch traced here: 65.2 us
  Pallas kernels  59.9 us (92%)
  local copies, waits for them, and re-layouts  4.73 us (7%)
    pallas_call x1, Pallas kernels, per_device(): pl.pallas_call(kernel, out_shape=(jax.ShapeDtypeStruct(particle_distribut...  59.9 us
    unnamed x8, local copies, waits for them, and re-layouts  4.73 us

profile of v1, /device:TPU:1, one launch (start us, length us, event | category | flops | bytes accessed | tf_op | source)
XLA Modules:
  0.0 65.2 jit_solution(14950299765041197144)
XLA Ops:
  0.6 0.0 copy-start
  0.6 1.6 %copy-done = f32[128,32,128]{2,1,0:T(8,128)S(1)} copy-done((f32[128,32,128]{2,1,0:T(8,128)S(1)}, f32[128,32,128]{2,1,0:T(8,128)}, u32[]{:S(2)}) %copy-start) | copy-done | bytes 2097176
  2.2 0.0 copy-start.1
  2.2 0.7 %copy-done.1 = f32[16]{0:T(128)S(1)} copy-done((f32[16]{0:T(128)S(1)}, f32[16]{0:T(128)}, u32[]{:S(2)}) %copy-start.1) | copy-done | bytes 88
  2.9 0.0 copy-start.2
  2.9 0.7 %copy-done.2 = s32[128]{0:T(128)S(1)} copy-done((s32[128]{0:T(128)S(1)}, s32[128]{0:T(128)}, u32[]{:S(2)}) %copy-start.2) | copy-done | bytes 536
  3.5 59.9 %shard_map.50 = (f32[128,32,128]{2,1,0:T(8,128)S(1)}, f32[1,16]{1,0:T(1,128)S(1)}) custom-call(f32[128,32,128]{2,1,0:T(8,128)S(1)} %copy-done, f32[1,16]{1,0:T(1,128)S(1)} %bitcast.3, s32[1,128]{1,0:T(1,128)S(1)} %bitcast.4), custom_call_target="tpu_custom_call" | custom-call | tf_op jit(solution)/shard_map/pallas_call | solution.py:599
  63.4 1.3 %copy.7 = f32[128,32,128]{2,1,0:T(8,128)} copy(f32[128,32,128]{2,1,0:T(8,128)S(1)} %get-tuple-element.8) | data formatting | bytes 4194304
  64.7 0.5 copy.8
Async XLA Ops:
  0.6 1.6 %copy-start = (f32[128,32,128]{2,1,0:T(8,128)S(1)}, f32[128,32,128]{2,1,0:T(8,128)}, u32[]{:S(2)}) copy-start(f32[128,32,128]{2,1,0:T(8,128)} %f_hbm.1) | copy-start | bytes 6291460
  2.2 0.7 %copy-start.1 = (f32[16]{0:T(128)S(1)}, f32[16]{0:T(128)}, u32[]{:S(2)}) copy-start(f32[16]{0:T(128)} %param.4) | copy-start | bytes 196
  2.9 0.7 %copy-start.2 = (s32[128]{0:T(128)S(1)}, s32[128]{0:T(128)}, u32[]{:S(2)}) copy-start(s32[128]{0:T(128)} %param.5) | copy-start | bytes 1540

commit v2 on v1

v2 whole, which is shorter than its diff:
```python
import functools
import math

import jax
import jax.numpy as jnp
from jax import lax
from jax.experimental import pallas as pl
from jax.experimental.pallas import tpu as pltpu
from jax.sharding import PartitionSpec as P

MESH = pl.DeviceIdType.MESH
N = 16
ROWS = 32
LANES = 128
TWO_PI = 2.0 * math.pi
BITREV = (0, 4, 2, 6, 1, 5, 3, 7)
F32 = jnp.float32


def iota(axis):
    return lax.broadcasted_iota(jnp.int32, (8, LANES), axis)


def spread(row):
    return jnp.broadcast_to(row, (8, LANES))


def minmod(p, q):
    return jnp.maximum(jnp.minimum(p, 0.0), jnp.minimum(jnp.maximum(p, 0.0), q))


def flip8(x, sub):
    x = pltpu.roll(x, 4, 0)
    x = jnp.where((sub & 2) == 0, pltpu.roll(x, 6, 0), pltpu.roll(x, 2, 0))
    return jnp.where((sub & 1) == 0, pltpu.roll(x, 7, 0), pltpu.roll(x, 1, 0))


def merge(a, b, h, sub):
    low = (sub & h) == 0
    if h == 4:
        return jnp.where(low, a, b) + pltpu.roll(jnp.where(low, b, a), 4, 0)
    return jnp.where(low, a, pltpu.roll(b, h, 0)) + jnp.where(
        low, pltpu.roll(a, 8 - h, 0), b
    )


def stack_sums(parts, sub):
    x = [parts[BITREV[i]] for i in range(8)]
    x = [merge(x[2 * i], x[2 * i + 1], 4, sub) for i in range(4)]
    x = [merge(x[2 * i], x[2 * i + 1], 2, sub) for i in range(2)]
    return merge(x[0], x[1], 1, sub)


def z_sums(v):
    s = [v[4 + j] + v[3 - j] for j in range(4)]
    d = [v[4 + j] - v[3 - j] for j in range(4)]
    total = (s[0] + s[1]) + (s[2] + s[3])
    first = (0.5 * d[0] + 1.5 * d[1]) + (2.5 * d[2] + 3.5 * d[3])
    second = (0.25 * s[0] + 2.25 * s[1]) + (6.25 * s[2] + 12.25 * s[3])
    return total, first, second


def quads(low, high, y):
    s0, z0, zz0 = z_sums(low)
    s1, z1, zz1 = z_sums(high)
    a0, a1 = y[0] * s0, y[1] * s1
    return (s0 + s1, a0 + a1, z0 + z1, (y[0] * a0 + y[1] * a1) + (zz0 + zz1)), (
        a1,
        y[1] * (y[1] * a1 + zz1),
    )


def gas(total, by_x, by_xx, sub, face):
    s0 = total
    ux = by_x / s0
    uy = pltpu.roll(total, 6, 0) / s0
    uz = pltpu.roll(total, 4, 0) / s0
    rho = 0.25 * s0
    temp = ((by_xx + pltpu.roll(total, 2, 0)) / s0 - (ux * ux + uy * uy + uz * uz)) / 3.0
    tau = 8.0 * jnp.exp(-0.19 * jnp.log(temp)) / rho
    if face:
        mix = 2.0 * tau / (2.0 * tau + 0.125)
        share = 0.125 / (2.0 * tau + 0.125)
    else:
        mix = (2.0 * tau - 0.125) / (2.0 * tau + 0.25)
        share = 0.375 / (2.0 * tau + 0.25)
    weight = share * rho * jnp.exp(-1.5 * jnp.log(TWO_PI * temp))
    half = 0.5 / temp
    first = jnp.where(
        sub < 2,
        mix,
        jnp.where(
            sub < 4,
            pltpu.roll(weight, 2, 0),
            jnp.where(sub < 6, pltpu.roll(ux, 4, 0), pltpu.roll(uy, 6, 0)),
        ),
    )
    second = jnp.where(sub < 2, uz, pltpu.roll(half, 2, 0))
    return first, second


def gather_sums(ref):
    total = by_x = by_xx = None
    for k in range(N):
        x = 0.5 * (k - 7.5)
        t = ref[k]
        if k == 0:
            total, by_x, by_xx = t, x * t, (x * x) * t
        else:
            total, by_x, by_xx = total + t, by_x + x * t, by_xx + (x * x) * t
    return total, by_x, by_xx


def factors(first, second, row, y, zed, xi_x):
    mix = spread(first[0 + row : 1 + row])
    weight = spread(first[2 + row : 3 + row])
    ux = spread(first[4 + row : 5 + row])
    uy = spread(first[6 + row : 7 + row])
    uz = spread(second[0 + row : 1 + row])
    half = spread(second[2 + row : 3 + row])
    ey = [jnp.exp(-((y[h] - uy) * (y[h] - uy)) * half) for h in range(2)]
    dz, dx = zed - uz, xi_x - ux
    bz = weight * jnp.exp(-(dz * dz + dx * dx) * half)
    return mix, ey, bz


def velocities():
    subf = iota(0).astype(F32)
    return (0.5 * (subf - 7.5), 0.5 * (subf + 0.5)), subf - 3.5


def y_flux(first, second, row, g, j, xi_x):
    y, zed = velocities()
    mix, ey, bz = factors(first, second, row, y, zed, xi_x)
    out = []
    mixed = [mix * (0.25 * y[h]) for h in range(2)]
    eyed = [ey[h] * (0.25 * y[h]) for h in range(2)]
    for iz in range(8):
        b = spread(bz[iz : iz + 1])
        for h in range(2):
            out.append(mixed[h] * g[j, pl.ds(iz * 16 + h * 8, 8), :] + eyed[h] * b)
    return out


def kernel(
    f_hbm, pw_hbm, lab_hbm,
    out_hbm, rev_hbm,
    fv, gy, ay, wf, rev_ref, plus, gx, pw_ref, lab_ref,
    s1, r1, a1, sx, rx, ax, sy, ry, s32, r32, sex, rex, shs, rhs,
    warm, heat, pk, pku, pkd, hf, cpk, gpk, x8_ref, fx_ref, fp_ref, prev,
    in_sem, out_sem, send, recv, arrive, hsend, hrecv,
):
    me = lax.axis_index("vel")
    sp = lax.axis_index("space")
    ip = (me >= 8).astype(jnp.int32)
    dirn = 2 * ip - 1
    xi_x = 0.5 * (me.astype(F32) - 7.5)
    abs_x = xi_x * dirn.astype(F32)
    sub, lane = iota(0), iota(1)
    y, zed = velocities()
    step_dn = lax.rem(dirn + 128, 128)
    step_up = lax.rem(128 - dirn, 128)
    at_up = lane == 127 - 127 * ip
    at_dn = lane == 127 * ip
    is_pos = lane < 128 * ip
    zero = jnp.zeros((8, LANES), F32)

    def far(i):
        half = i // 2
        return 8 + jnp.where(lax.rem(i, 2) == 0, -half, half)

    def near(i):
        half = (i + 1) // 2
        return lax.rem(jnp.where(lax.rem(i, 2) == 0, N - half, half), N)

    def vel_copy(group, d, src, dst, each=None):
        return pltpu.make_async_remote_copy(
            src, dst, send.at[group], recv.at[group] if each is None else arrive.at[each, d],
            device_id={"vel": lax.rem(me + d, N)}, device_id_type=MESH,
        )

    def space_copy(group, d, src, dst):
        return pltpu.make_async_remote_copy(
            src, dst, hsend.at[group], hrecv.at[group],
            device_id={"space": lax.rem(sp + d, N)}, device_id_type=MESH,
        )

    def drain(sem, buf):
        part = buf.at[pl.ds(0, N - 1)]
        pltpu.make_async_copy(part, part, sem).wait()

    def arrival(each, d, buf):
        src = lax.rem(me - d + N, N)
        pltpu.make_async_copy(buf.at[src], buf.at[src], arrive.at[each, d]).wait()

    barrier = pltpu.get_barrier_semaphore()

    @pl.loop(1, N)
    def _(i):
        d = far(i)
        pl.semaphore_signal(
            barrier, 1, device_id={"vel": lax.rem(me + d, N)}, device_id_type=MESH
        )
        pl.semaphore_signal(
            barrier, 1, device_id={"space": lax.rem(sp + d, N)}, device_id_type=MESH
        )

    pw_copy = pltpu.make_async_copy(pw_hbm, pw_ref, in_sem.at[ROWS])
    lab_copy = pltpu.make_async_copy(lab_hbm, lab_ref, in_sem.at[ROWS + 1])
    pw_copy.start()
    lab_copy.start()
    for r in range(ROWS):
        pltpu.make_async_copy(f_hbm.at[:, r], fv.at[r], in_sem.at[r]).start()
    for i in range(16):
        pk[i] = zero

    pw_copy.wait()
    lab_copy.wait()
    own = jnp.broadcast_to(pw_ref[...], (16, 16))
    diag = lax.broadcasted_iota(jnp.int32, (16, 16), 0) == lax.broadcasted_iota(
        jnp.int32, (16, 16), 1
    )
    own = jnp.sum(jnp.where(diag, own, 0.0), axis=1, keepdims=True)
    warm[sp] = jnp.broadcast_to(own, (16, LANES))

    @pl.loop(0, N)
    def _(o):
        parts = [None] * 8
        for row in range(2):
            r = 2 * o + row
            pltpu.make_async_copy(f_hbm.at[:, r], fv.at[r], in_sem.at[r]).wait()
            shift = 4 * r + 2
            mask = (lane >= 4 * r) & (lane <= 4 * r + 3)
            v = [[None] * 8, [None] * 8]
            for iz in range(8):
                for h in range(2):
                    t = fv[r, pl.ds(iz * 16 + h * 8, 8), :]
                    v[h][iz] = t
                    i = iz * 2 + h
                    pk[i] = jnp.where(mask, pltpu.roll(t, shift, 1), pk[i])
            q, _w = quads(v[0], v[1], y)
            for i in range(4):
                parts[2 * i + row] = q[i]
        s1[o] = stack_sums(parts, sub)

    r1[me] = s1[me]
    pl.semaphore_wait(barrier, 2 * (N - 1))

    @pl.loop(1, N)
    def _(i):
        d = far(i)
        vel_copy(0, d, s1.at[lax.rem(me + d, N)], r1.at[me]).start()

    to_down = pltpu.make_async_remote_copy(
        pk, pku, hsend.at[2], hrecv.at[2],
        device_id={"space": lax.rem(sp + dirn + N, N)}, device_id_type=MESH,
    )
    to_up = pltpu.make_async_remote_copy(
        pk, pkd, hsend.at[3], hrecv.at[3],
        device_id={"space": lax.rem(sp - dirn + N, N)}, device_id_type=MESH,
    )
    to_down.start()
    to_up.start()

    @pl.loop(1, N)
    def _(d):
        space_copy(0, d, warm.at[sp], warm.at[sp]).start()

    to_down.wait_recv()
    to_up.wait_recv()
    v = [[None] * 8, [None] * 8]
    w = [[None] * 8, [None] * 8]
    left = ((lane & 2) == 0) == is_pos
    for iz in range(8):
        for h in range(2):
            i = iz * 2 + h
            t = jnp.where(left, pku[i], pkd[i])
            hf[i] = t
            v[h][iz] = t
            w[h][iz] = pk[i]
    q, _w = quads(v[0], v[1], y)
    p, _w = quads(w[0], w[1], y)
    shs[...] = stack_sums([q[0], p[0], q[1], p[1], q[2], p[2], q[3], p[3]], sub)
    rhs[me] = shs[...]

    @pl.loop(1, N)
    def _(i):
        vel_copy(1, far(i), shs, rhs.at[me]).start()

    drain(recv.at[0], r1)
    first, second = gas(*gather_sums(r1), sub, False)
    a1[me, 0:8, :] = first
    a1[me, 8:12, :] = second[0:4]

    @pl.loop(1, N)
    def _(i):
        vel_copy(2, far(i), a1.at[me], a1.at[me], 0).start()

    drain(recv.at[1], rhs)
    first, second = gas(*gather_sums(rhs), sub, False)
    cx = 0.5 - 0.125 * abs_x
    quarter = lane & 3
    centre = quarter == 2 - ip
    across = lax.rem(128 - 2 * dirn, 128)
    sets = []
    for row in range(2):
        mix, weight, ux, uy = [spread(first[2 * i + row : 2 * i + row + 1]) for i in range(4)]
        uz, half = spread(second[row : row + 1]), spread(second[2 + row : 3 + row])
        ey = [jnp.exp(-((y[h] - uy) * (y[h] - uy)) * half) for h in range(2)]
        sets.append((mix, weight, ux - xi_x, uz, half, ey))
    v = [[None] * 8, [None] * 8]
    for iz in range(8):
        b = []
        for mix, weight, dx, uz, half, ey in sets:
            dz = (iz - 3.5) - uz
            b.append(weight * jnp.exp(-(dz * dz + dx * dx) * half))
        for h in range(2):
            i = iz * 2 + h
            u = sets[0][0] * hf[i] + sets[0][5][h] * b[0]
            inside = sets[1][0] * pk[i] + sets[1][5][h] * b[1]
            u2 = pltpu.roll(u, step_dn, 1)
            w0 = pltpu.roll(inside, step_up, 1)
            g = u + cx * minmod(w0 - u, u - u2)
            gpk[i] = g
            v[h][iz] = g
            cpk[i] = jnp.where(centre, u, pltpu.roll(u, across, 1))
    q, _w = quads(v[0], v[1], y)
    parts = [None] * 8
    for k in range(4):
        parts[2 * k] = q[k]
        parts[2 * k + 1] = pltpu.roll(q[k], 124, 1)
    x8 = pltpu.roll(stack_sums(parts, sub), lax.rem(127 + ip, 128), 1)
    x8_ref[...] = x8
    sex[...] = jnp.where(is_pos, 0.0, x8)
    drain(send.at[0], r1)
    drain(send.at[1], rhs)
    to_down.wait_send()
    to_up.wait_send()

    @pl.loop(0, N)
    def _(i):
        d = near(i)
        o = lax.rem(me - d + N, N)

        @pl.when(i > 0)
        def _():
            arrival(0, d, a1)

        first, second = a1[o, 0:8, :], a1[o, 8:12, :]
        parts = [None] * 8
        for row in range(2):
            r = 2 * o + row
            mix, ey, bz = factors(first, second, row, y, zed, xi_x)
            shift = 125 - 4 * r + 2 * ip
            v = [[None] * 8, [None] * 8]
            for iz in range(8):
                b = spread(bz[iz : iz + 1])
                for h in range(2):
                    at = pl.ds(iz * 16 + h * 8, 8)
                    p = mix * fv[r, at, :] + ey[h] * b
                    plus[r + 2, at, :] = p
                    edge = pltpu.roll(cpk[iz * 2 + h], shift, 1)
                    behind = jnp.where(at_up, edge, pltpu.roll(p, step_dn, 1))
                    ahead = jnp.where(at_dn, edge, pltpu.roll(p, step_up, 1))
                    g = p + cx * minmod(ahead - p, p - behind)
                    gx[r, at, :] = g
                    v[h][iz] = g
            q, _w = quads(v[0], v[1], y)
            for k in range(4):
                parts[2 * k + row] = q[k]
        t = stack_sums(parts, sub)
        at_o = (lane == 8 * o + 1) & is_pos
        sex[...] = jnp.where(at_o, pltpu.roll(t, 8 * o + 2, 1), sex[...])
        sx[o] = jnp.where(
            lane < ip, pltpu.roll(x8_ref[...], 127 - 8 * o, 1), pltpu.roll(t, ip, 1)
        )

        @pl.when(i > 0)
        def _():
            vel_copy(3, lax.rem(N - d, N), sx.at[o], rx.at[me]).start()

    rx[me] = sx[me]
    rex[me] = sex[...]

    for ghost, real in ((1, 2), (0, 3), (34, 33), (35, 32)):
        for iz in range(8):
            lo, hi = pl.ds(iz * 16, 8), pl.ds(iz * 16 + 8, 8)
            x0, x1 = plus[real, lo, :], plus[real, hi, :]
            plus[ghost, lo, :] = flip8(x1, sub)
            plus[ghost, hi, :] = flip8(x0, sub)

    cy = (0.5 + 0.125 * y[0], 0.5 - 0.125 * y[1])

    def y_face(j):
        v = [[None] * 8, [None] * 8]
        for iz in range(8):
            for h in range(2):
                at = pl.ds(iz * 16 + h * 8, 8)
                if h:
                    c, b, a = plus[j + 1, at, :], plus[j, at, :], plus[j + 2, at, :]
                else:
                    c, b, a = plus[j + 2, at, :], plus[j + 3, at, :], plus[j + 1, at, :]
                g = c + cy[h] * minmod(a - c, c - b)
                gy[j, at, :] = g
                v[h][iz] = g
        return quads(v[0], v[1], y)

    @pl.loop(0, N)
    def _(i):
        d = lax.rem(far(i + 1), N)
        o = lax.rem(me + d, N)
        parts = [None] * 8
        for row in range(2):
            q, _w = y_face(2 * o + row)
            for k in range(4):
                parts[2 * k + row] = q[k]
        sy[o] = stack_sums(parts, sub)

        @pl.when(d > 0)
        def _():
            vel_copy(4, d, sy.at[o], ry.at[me]).start()

    ry[me] = sy[me]
    q, w = y_face(32)
    s32[...] = stack_sums([q[0], w[0], q[1], w[1], q[2], zero, q[3], zero], sub)
    r32[me] = s32[...]

    @pl.loop(1, N)
    def _(i):
        d = far(i)
        vel_copy(5, d, s32, r32.at[me]).start()
        vel_copy(6, d, sex, rex.at[me]).start()

    @pl.loop(0, ROWS)
    def _(r):
        for i in range(16):
            at = pl.ds(i * 8, 8)
            fv[r, at, :] = (4.0 / 3.0) * plus[r + 2, at, :] - fv[r, at, :] * (1.0 / 3.0)

    drain(send.at[2], a1)
    drain(send.at[3], rx)

    drain(recv.at[3], rx)
    first, second = gas(*gather_sums(rx), sub, True)
    ax[me, 0:8, :] = first
    ax[me, 8:12, :] = second[0:4]

    @pl.loop(1, N)
    def _(i):
        vel_copy(7, far(i), ax.at[me], ax.at[me]).start()

    drain(recv.at[4], ry)
    first, second = gas(*gather_sums(ry), sub, True)
    ay[me, 0:8, :] = first
    ay[me, 8:12, :] = second[0:4]

    @pl.loop(1, N)
    def _(i):
        vel_copy(8, far(i), ay.at[me], ay.at[me]).start()

    drain(hrecv.at[0], warm)
    label = spread(lab_ref[...])
    walled = label >= 0
    tw_sum = zero
    for k in range(N):
        for h in range(2):
            tw_sum = tw_sum + jnp.where(
                label == k * 16 + h * 8 + sub, warm[k, pl.ds(8 * h, 8), :], 0.0
            )
    tw = jnp.where(walled, spread(jnp.sum(tw_sum, axis=0, keepdims=True)), 1.0)
    half_tw = 0.5 / tw
    wall_norm = jnp.exp(-1.5 * jnp.log(TWO_PI * tw))
    e_xy = jnp.exp(-(y[1] * y[1]) * half_tw)
    e_z = jnp.exp(-(zed * zed) * half_tw)

    def down(t):
        return spread(jnp.sum(t, axis=0, keepdims=True))

    sum_x, sum_xx = 2.0 * down(e_xy), 2.0 * down(y[1] * y[1] * e_xy)
    sum_z, sum_zz = down(e_z), down(zed * zed * e_z)
    sum_y1, sum_y3 = down(y[1] * e_xy), down(y[1] * y[1] * y[1] * e_xy)
    out_mass = wall_norm * (sum_x * sum_z * sum_y1)
    out_energy = 0.5 * wall_norm * (
        sum_xx * sum_z * sum_y1 + sum_x * sum_zz * sum_y1 + sum_x * sum_z * sum_y3
    )

    drain(recv.at[5], r32)
    total, by_x, by_xx = gather_sums(r32)
    wall_first, wall_second = gas(total, by_x, by_xx, sub, True)
    in_mass = spread(total[1:2])
    in_energy = 0.5 * spread(by_xx[1:2] + total[3:4])
    rho_w = in_mass / out_mass
    flow = jnp.where(walled, 0.25 * (in_energy - rho_w * out_energy), 0.0)
    heat[sp] = jnp.where(sub == 0, flow, label.astype(F32))

    @pl.loop(1, N)
    def _(d):
        space_copy(1, d, heat.at[sp], heat.at[sp]).start()

    flux = y_flux(wall_first, wall_second, 0, gy, 32, xi_x)
    ey_w = jnp.exp(-(y[0] * y[0]) * half_tw) * (0.25 * y[0])
    bz_w = rho_w * wall_norm * jnp.exp(-(zed * zed + xi_x * xi_x) * half_tw)
    for iz in range(8):
        b = spread(bz_w[iz : iz + 1])
        wf[2 * iz] = jnp.where(walled, ey_w * b, flux[2 * iz])
        wf[2 * iz + 1] = jnp.where(
            walled, (0.25 * y[1]) * gy[32, pl.ds(iz * 16 + 8, 8), :], flux[2 * iz + 1]
        )

    drain(recv.at[6], rex)
    fx_first, fx_second = gas(*gather_sums(rex), sub, True)
    fx_ref[0:8, :] = fx_first
    fx_ref[8:16, :] = fx_second
    drain(send.at[4], ry)
    drain(send.at[5], r32)
    drain(send.at[6], rex)
    drain(hsend.at[0], warm)

    drain(recv.at[7], ax)
    fp_ref[0:8, :] = jnp.where(is_pos, 0.0, fx_ref[0:8, :])
    fp_ref[8:12, :] = jnp.where(is_pos[0:4], 0.0, fx_ref[8:12, :])

    @pl.loop(0, N)
    def _(o):
        at_o = (lane == 8 * o + 1) & is_pos
        for lo, hi in ((0, 8), (8, 12)):
            fp_ref[lo:hi, :] = jnp.where(
                at_o[0 : hi - lo], pltpu.roll(ax[o, lo:hi, :], 8 * o + 1, 1), fp_ref[lo:hi, :]
            )

    quarter_x = 0.25 * abs_x
    fp = pltpu.roll(fp_ref[...], 1 - ip, 1)
    even = (lane & 7) == 2 - ip

    def packed(i):
        return jnp.where(
            even, spread(fp[i : i + 1]), pltpu.roll(spread(fp[i + 1 : i + 2]), 4, 1)
        )

    mix, weight, ux, uy, uz, half = [packed(2 * i) for i in range(6)]
    ey = [jnp.exp(-((y[h] - uy) * (y[h] - uy)) * half) for h in range(2)]
    dx = xi_x - ux
    for iz in range(8):
        dz = (iz - 3.5) - uz
        b = quarter_x * weight * jnp.exp(-(dz * dz + dx * dx) * half)
        for h in range(2):
            i = iz * 2 + h
            gpk[i] = (quarter_x * mix) * gpk[i] + ey[h] * b

    @pl.loop(0, N)
    def _(o):
        field = []
        for lo, hi in ((0, 8), (8, 12)):
            field.append(
                jnp.where(
                    ((lane == 127) & is_pos)[0 : hi - lo],
                    pltpu.roll(fx_ref[lo:hi, :], 126 - 8 * o, 1),
                    pltpu.roll(ax[o, lo:hi, :], lax.rem(128 - ip, 128), 1),
                )
            )
        for row in range(2):
            r = 2 * o + row
            shift = 125 - 4 * r + 2 * ip
            mix, ey, bz = factors(field[0], field[1], row, y, zed, xi_x)
            mix = quarter_x * mix
            bz = quarter_x * bz
            for iz in range(8):
                b = spread(bz[iz : iz + 1])
                for h in range(2):
                    at = pl.ds(iz * 16 + h * 8, 8)
                    flux = mix * gx[r, at, :] + ey[h] * b
                    edge = pltpu.roll(gpk[iz * 2 + h], shift, 1)
                    before = jnp.where(at_up, edge, pltpu.roll(flux, step_dn, 1))
                    fv[r, at, :] = fv[r, at, :] - (flux - before)

    drain(hrecv.at[1], heat)
    piece = lax.broadcasted_iota(jnp.int32, (16, LANES), 0) + sp * 16
    piecef = piece.astype(F32)
    gained = jnp.zeros((16, LANES), F32)
    for k in range(N):
        t = heat[k]
        gained = gained + jnp.where(
            jnp.broadcast_to(t[1:2], (16, LANES)) == piecef,
            jnp.broadcast_to(t[0:1], (16, LANES)),
            0.0,
        )
    gained = jnp.sum(gained, axis=1, keepdims=True)
    own = warm[sp]
    dev = own - 1.0
    before = jnp.where(sp == 0, 0.0, 1.0) * (warm[lax.rem(sp + N - 1, N), 15:16, :] - 1.0)
    after = jnp.where(sp == N - 1, 0.0, 1.0) * (warm[lax.rem(sp + 1, N), 0:1, :] - 1.0)
    dev_before = jnp.concatenate([before, dev[:-1]], axis=0)
    dev_after = jnp.concatenate([dev[1:], after], axis=0)
    new = own + 0.45 * (dev_before - 2.0 * dev + dev_after) + 0.025 * gained
    on_diag = lax.broadcasted_iota(jnp.int32, (16, LANES), 1) == lax.broadcasted_iota(
        jnp.int32, (16, LANES), 0
    )
    rev_ref[...] = jnp.sum(jnp.where(on_diag, new, 0.0), axis=0, keepdims=True)[:, 0:16]

    rev_copy = pltpu.make_async_copy(rev_ref, rev_hbm, out_sem.at[ROWS])
    rev_copy.start()
    drain(send.at[7], ax)
    drain(hsend.at[1], heat)

    drain(recv.at[8], ay)
    def update(r, flux):
        for i in range(16):
            at = pl.ds(i * 8, 8)
            gx[r, at, :] = fv[r, at, :] - (flux[i] - prev[i])
            prev[i] = flux[i]
        pltpu.make_async_copy(gx.at[r], out_hbm.at[:, r], out_sem.at[r]).start()

    def face(o, row):
        return y_flux(ay[o, 0:8, :], ay[o, 8:12, :], row, gy, 2 * o + row, xi_x)

    flux = face(0, 0)
    for i in range(16):
        prev[i] = flux[i]

    @pl.loop(0, N - 1)
    def _(o):
        update(2 * o, face(o, 1))
        update(2 * o + 1, face(o + 1, 0))

    update(30, face(N - 1, 1))
    update(31, [wf[i] for i in range(16)])
    drain(send.at[8], ay)
    rev_copy.wait()

    @pl.loop(0, ROWS)
    def _(r):
        pltpu.make_async_copy(gx.at[r], out_hbm.at[:, r], out_sem.at[r]).wait()


def per_device(particle_distribution, piece_warmth, exterior_piece_label):
    tile = functools.partial(pltpu.VMEM, dtype=F32)
    dma = pltpu.SemaphoreType.DMA
    hbm = pl.BlockSpec(memory_space=pltpu.HBM)
    one = tile((N, 8, LANES))
    two = tile((N, 12, LANES))
    flat = tile((8, LANES))
    shape = functools.partial(jax.ShapeDtypeStruct, dtype=F32)
    out, revised = pl.pallas_call(
        kernel,
        out_shape=(shape(particle_distribution.shape), shape((1, 16))),
        in_specs=[hbm] * 3,
        out_specs=(hbm, hbm),
        scratch_shapes=[
            tile((ROWS, 128, LANES)), tile((ROWS + 1, 128, LANES)), two, one, tile((1, 16)),
            tile((ROWS + 4, 128, LANES)), tile((ROWS, 128, LANES)),
            tile((1, 16)), pltpu.VMEM((1, LANES), jnp.int32),
            one, one, two,
            one, one, two,
            one, one,
            flat, one,
            flat, one,
            flat, one,
            tile((N, 16, LANES)), one,
            one, one, one, one, one, one,
            flat, tile((16, LANES)), tile((12, LANES)), one,
            dma((ROWS + 2,)), dma((ROWS + 1,)),
            dma((9,)), dma((9,)), dma((1, N)), dma((4,)), dma((4,)),
        ],
        compiler_params=pltpu.CompilerParams(
            collective_id=0, has_side_effects=True, vmem_limit_bytes=62 * 1024 * 1000
        ),
    )(
        particle_distribution,
        piece_warmth.reshape(1, 16),
        exterior_piece_label.reshape(1, LANES),
    )
    return out, revised.reshape(16)


def solution(mesh):
    return jax.shard_map(
        per_device,
        mesh=mesh,
        in_specs=(P("vel", None, "space"), P("space"), P("space")),
        out_specs=(P("vel", None, "space"), P("space")),
        check_vma=False,
    )
```

time: 65.4 us -> 49.2 us (0.75)
  Pallas kernels: 59.9 us -> 44.8 us
  local copies, waits for them, and re-layouts: 4.73 us -> 3.6 us
    pallas_call x1, Pallas kernels: 59.9 us -> 44.8 us  [per_device(): pl.pallas_call(kernel, out_shape=(shape(particle_distribution.shape), sha...]
    unnamed x8 -> x4, local copies, waits for them, and re-layouts: 4.73 us -> 3.6 us
where the time goes in v2:
time: 49.2 us; the launch traced here: 49 us
  Pallas kernels  44.8 us (91%)
  local copies, waits for them, and re-layouts  3.6 us (7%)
  between operations  0.65 us (1%)
    pallas_call x1, Pallas kernels, per_device(): pl.pallas_call(kernel, out_shape=(shape(particle_distribution.shape), sha...  44.8 us
    unnamed x4, local copies, waits for them, and re-layouts  3.6 us

profile of v2, /device:TPU:1, one launch (start us, length us, event | category | flops | bytes accessed | tf_op | source)
XLA Modules:
  0.0 49.0 jit_solution(16003044424448464796)
XLA Ops:
  0.6 44.8 %shard_map.50 = (f32[128,32,128]{2,1,0:T(8,128)}, f32[1,16]{1,0:T(1,128)}) custom-call(f32[128,32,128]{2,1,0:T(8,128)} %f_hbm.1, f32[1,16]{1,0:T(1,128)} %bitcast.3, s32[1,128]{1,0:T(1,128)} %bitcast.4), custom_call_target="tpu_custom_call" | custom-call | tf_op jit(solution)/shard_map/pallas_call | solution.py:643
  45.4 0.0 copy-start
  45.4 3.1 %copy.7 = f32[128,32,128]{2,1,0:T(8,128)} copy(f32[128,32,128]{2,1,0:T(8,128)} %get-tuple-element.8) | data formatting | bytes 4194304
  48.5 0.0 copy-done
  48.5 0.5 %copy.8 = f32[16]{0:T(128)} copy(f32[16]{0:T(128)S(1)} %bitcast.5) | data formatting | bytes 128
Async XLA Ops:
  45.4 3.1 %copy-start = (f32[1,16]{1,0:T(1,128)S(1)}, f32[1,16]{1,0:T(1,128)}, u32[]{:S(2)}) copy-start(f32[1,16]{1,0:T(1,128)} %get-tuple-element.5) | copy-start | bytes 196

commit v3 on v2

v3 whole, which is shorter than its diff:
```python
import functools
import math

import jax
import jax.numpy as jnp
from jax import lax
from jax.experimental import pallas as pl
from jax.experimental.pallas import tpu as pltpu
from jax.sharding import PartitionSpec as P

MESH = pl.DeviceIdType.MESH
N = 16
ROWS = 32
LANES = 128
TWO_PI = 2.0 * math.pi
BITREV = (0, 4, 2, 6, 1, 5, 3, 7)
F32 = jnp.float32


def iota(axis):
    return lax.broadcasted_iota(jnp.int32, (8, LANES), axis)


def spread(row):
    return jnp.broadcast_to(row, (8, LANES))


def minmod(p, q):
    return jnp.maximum(jnp.minimum(p, 0.0), jnp.minimum(jnp.maximum(p, 0.0), q))


def flip8(x, sub):
    x = pltpu.roll(x, 4, 0)
    x = jnp.where((sub & 2) == 0, pltpu.roll(x, 6, 0), pltpu.roll(x, 2, 0))
    return jnp.where((sub & 1) == 0, pltpu.roll(x, 7, 0), pltpu.roll(x, 1, 0))


def merge(a, b, h, sub):
    low = (sub & h) == 0
    if h == 4:
        return jnp.where(low, a, b) + pltpu.roll(jnp.where(low, b, a), 4, 0)
    return jnp.where(low, a, pltpu.roll(b, h, 0)) + jnp.where(
        low, pltpu.roll(a, 8 - h, 0), b
    )


def stack_sums(parts, sub):
    x = [parts[BITREV[i]] for i in range(8)]
    x = [merge(x[2 * i], x[2 * i + 1], 4, sub) for i in range(4)]
    x = [merge(x[2 * i], x[2 * i + 1], 2, sub) for i in range(2)]
    return merge(x[0], x[1], 1, sub)


def z_sums(v):
    s = [v[4 + j] + v[3 - j] for j in range(4)]
    d = [v[4 + j] - v[3 - j] for j in range(4)]
    total = (s[0] + s[1]) + (s[2] + s[3])
    first = (0.5 * d[0] + 1.5 * d[1]) + (2.5 * d[2] + 3.5 * d[3])
    second = (0.25 * s[0] + 2.25 * s[1]) + (6.25 * s[2] + 12.25 * s[3])
    return total, first, second


def quads(low, high, y):
    s0, z0, zz0 = z_sums(low)
    s1, z1, zz1 = z_sums(high)
    a0, a1 = y[0] * s0, y[1] * s1
    return (s0 + s1, a0 + a1, z0 + z1, (y[0] * a0 + y[1] * a1) + (zz0 + zz1)), (
        a1,
        y[1] * (y[1] * a1 + zz1),
    )


def gas(total, by_x, by_xx, sub, face):
    s0 = total
    ux = by_x / s0
    uy = pltpu.roll(total, 6, 0) / s0
    uz = pltpu.roll(total, 4, 0) / s0
    rho = 0.25 * s0
    temp = ((by_xx + pltpu.roll(total, 2, 0)) / s0 - (ux * ux + uy * uy + uz * uz)) / 3.0
    tau = 8.0 * jnp.exp(-0.19 * jnp.log(temp)) / rho
    if face:
        mix = 2.0 * tau / (2.0 * tau + 0.125)
        share = 0.125 / (2.0 * tau + 0.125)
    else:
        mix = (2.0 * tau - 0.125) / (2.0 * tau + 0.25)
        share = 0.375 / (2.0 * tau + 0.25)
    weight = share * rho * jnp.exp(-1.5 * jnp.log(TWO_PI * temp))
    half = 0.5 / temp
    first = jnp.where(
        sub < 2,
        mix,
        jnp.where(
            sub < 4,
            pltpu.roll(weight, 2, 0),
            jnp.where(sub < 6, pltpu.roll(ux, 4, 0), pltpu.roll(uy, 6, 0)),
        ),
    )
    second = jnp.where(sub < 2, uz, pltpu.roll(half, 2, 0))
    return first, second


def gather_sums(ref):
    total = by_x = by_xx = None
    for k in range(N):
        x = 0.5 * (k - 7.5)
        t = ref[k]
        if k == 0:
            total, by_x, by_xx = t, x * t, (x * x) * t
        else:
            total, by_x, by_xx = total + t, by_x + x * t, by_xx + (x * x) * t
    return total, by_x, by_xx


def factors(first, second, row, y, zed, xi_x):
    mix = spread(first[0 + row : 1 + row])
    weight = spread(first[2 + row : 3 + row])
    ux = spread(first[4 + row : 5 + row])
    uy = spread(first[6 + row : 7 + row])
    uz = spread(second[0 + row : 1 + row])
    half = spread(second[2 + row : 3 + row])
    ey = [jnp.exp(-((y[h] - uy) * (y[h] - uy)) * half) for h in range(2)]
    dz, dx = zed - uz, xi_x - ux
    bz = weight * jnp.exp(-(dz * dz + dx * dx) * half)
    return mix, ey, bz


def velocities():
    subf = iota(0).astype(F32)
    return (0.5 * (subf - 7.5), 0.5 * (subf + 0.5)), subf - 3.5


def y_flux(first, second, row, g, j, xi_x):
    y, zed = velocities()
    mix, ey, bz = factors(first, second, row, y, zed, xi_x)
    out = []
    mixed = [mix * (0.25 * y[h]) for h in range(2)]
    eyed = [ey[h] * (0.25 * y[h]) for h in range(2)]
    for iz in range(8):
        b = spread(bz[iz : iz + 1])
        for h in range(2):
            out.append(mixed[h] * g[j, pl.ds(iz * 16 + h * 8, 8), :] + eyed[h] * b)
    return out


def kernel(
    f_hbm, pw_hbm, lab_hbm,
    out_hbm, rev_hbm,
    fv, gy, ay, wf, rev_ref, plus, gx, pw_ref, lab_ref,
    s1, r1, a1, sx, rx, ax, sy, ry, s32, r32, sex, rex, shs, rhs,
    warm, heat, pk, pku, pkd, hf, ge, gh, slots, fresh,
    in_sem, out_sem, send, recv, arrive, hsend, hrecv,
):
    me = lax.axis_index("vel")
    sp = lax.axis_index("space")
    ip = (me >= 8).astype(jnp.int32)
    dirn = 2 * ip - 1
    xi_x = 0.5 * (me.astype(F32) - 7.5)
    cx = 0.5 * dirn.astype(F32) - 0.125 * xi_x
    sub, lane = iota(0), iota(1)
    y, zed = velocities()
    is_pos = lane < 128 * ip
    at_edge = (lane == 0) | (lane == 127 - 126 * ip)
    zero = jnp.zeros((8, LANES), F32)

    def far(i):
        half = i // 2
        return 8 + jnp.where(lax.rem(i, 2) == 0, -half, half)

    def near(i):
        half = (i + 1) // 2
        return lax.rem(jnp.where(lax.rem(i, 2) == 0, N - half, half), N)

    def vel_copy(group, d, src, dst, each=None):
        return pltpu.make_async_remote_copy(
            src, dst, send.at[group], recv.at[group] if each is None else arrive.at[each, d],
            device_id={"vel": lax.rem(me + d, N)}, device_id_type=MESH,
        )

    def space_copy(group, d, src, dst):
        return pltpu.make_async_remote_copy(
            src, dst, hsend.at[group], hrecv.at[group],
            device_id={"space": lax.rem(sp + d, N)}, device_id_type=MESH,
        )

    def drain(sem, buf):
        part = buf.at[pl.ds(0, N - 1)]
        pltpu.make_async_copy(part, part, sem).wait()

    def arrival(each, d, buf):
        src = lax.rem(me - d + N, N)
        pltpu.make_async_copy(buf.at[src], buf.at[src], arrive.at[each, d]).wait()

    def load16(ref, r):
        return [
            [ref[r, pl.ds(iz * 16 + h * 8, 8), :] for iz in range(8)] for h in range(2)
        ]

    barrier = pltpu.get_barrier_semaphore()

    @pl.loop(1, N)
    def _(i):
        d = far(i)
        pl.semaphore_signal(
            barrier, 1, device_id={"vel": lax.rem(me + d, N)}, device_id_type=MESH
        )
        pl.semaphore_signal(
            barrier, 1, device_id={"space": lax.rem(sp + d, N)}, device_id_type=MESH
        )

    for r in range(ROWS):
        pltpu.make_async_copy(f_hbm.at[:, r], fv.at[r], in_sem.at[r]).start()
    pw_copy = pltpu.make_async_copy(pw_hbm, pw_ref, in_sem.at[ROWS])
    lab_copy = pltpu.make_async_copy(lab_hbm, lab_ref, in_sem.at[ROWS + 1])
    pw_copy.start()
    lab_copy.start()

    for i in range(16):
        pk[i] = zero

    @pl.loop(0, N)
    def _(o):
        parts = [None] * 8
        edge = [pk[i] for i in range(16)]
        for row in range(2):
            r = 2 * o + row
            pltpu.make_async_copy(f_hbm.at[:, r], fv.at[r], in_sem.at[r]).wait()
        for row in range(2):
            r = 2 * o + row
            v = load16(fv, r)
            mask = (lane >= 4 * r) & (lane <= 4 * r + 3)
            for i in range(16):
                edge[i] = jnp.where(mask, pltpu.roll(v[i % 2][i // 2], 4 * r + 2, 1), edge[i])
            q, _w = quads(v[0], v[1], y)
            for i in range(4):
                parts[2 * i + row] = q[i]
        for i in range(16):
            pk[i] = edge[i]
        s1[o] = stack_sums(parts, sub)

    r1[me] = s1[me]
    pl.semaphore_wait(barrier, 2 * (N - 1))

    @pl.loop(1, N)
    def _(i):
        d = far(i)
        vel_copy(0, d, s1.at[lax.rem(me + d, N)], r1.at[me]).start()

    to_right = pltpu.make_async_remote_copy(
        pk, pku, hsend.at[2], hrecv.at[2],
        device_id={"space": lax.rem(sp + 1, N)}, device_id_type=MESH,
    )
    to_left = pltpu.make_async_remote_copy(
        pk, pkd, hsend.at[3], hrecv.at[3],
        device_id={"space": lax.rem(sp + N - 1, N)}, device_id_type=MESH,
    )
    to_right.start()
    to_left.start()

    drain(recv.at[0], r1)
    first, second = gas(*gather_sums(r1), sub, False)
    a1[me, 0:8, :] = first
    a1[me, 8:12, :] = second[0:4]

    @pl.loop(1, N)
    def _(i):
        vel_copy(2, far(i), a1.at[me], a1.at[me], 0).start()

    to_right.wait_recv()
    to_left.wait_recv()
    v = [[None] * 8, [None] * 8]
    w = [[None] * 8, [None] * 8]
    for iz in range(8):
        for h in range(2):
            i = iz * 2 + h
            t = jnp.where((lane & 2) == 0, pku[i], pkd[i])
            hf[i] = t
            v[h][iz] = t
            w[h][iz] = pk[i]
    q, _w = quads(v[0], v[1], y)
    p, _w = quads(w[0], w[1], y)
    shs[...] = stack_sums([q[0], p[0], q[1], p[1], q[2], p[2], q[3], p[3]], sub)
    rhs[me] = shs[...]

    @pl.loop(1, N)
    def _(i):
        vel_copy(1, far(i), shs, rhs.at[me]).start()

    pw_copy.wait()
    lab_copy.wait()
    warm[sp, :, 0:16] = pw_ref[...]

    @pl.loop(1, N)
    def _(d):
        space_copy(0, d, warm.at[sp], warm.at[sp]).start()

    drain(send.at[0], r1)

    def owner(i):
        return lax.rem(me - near(i) + N, N)

    def half_step(i, slot):
        o = owner(i)
        first, second = a1[o, 0:8, :], a1[o, 8:12, :]
        for row in range(2):
            r = 2 * o + row
            mix, ey, bz = factors(first, second, row, y, zed, xi_x)
            for iz in range(8):
                b = spread(bz[iz : iz + 1])
                for h in range(2):
                    at = pl.ds(iz * 16 + h * 8, 8)
                    p = mix * fv[r, at, :] + ey[h] * b
                    plus[r + 2, at, :] = p
                    fresh[slot, row, at, :] = p

    def rolls(slot):
        for row in range(2):
            for k in range(16):
                at = pl.ds(k * 8, 8)
                p = fresh[slot, row, at, :]
                slots[slot, 0, row, at, :] = p
                slots[slot, 1, row, at, :] = pltpu.roll(p, 1, 1)
                slots[slot, 2, row, at, :] = pltpu.roll(p, 127, 1)

    def x_faces(i, slot):
        o = owner(i)
        parts = [None] * 8
        for row in range(2):
            r = 2 * o + row
            v = [[None] * 8, [None] * 8]
            for iz in range(8):
                for h in range(2):
                    at = pl.ds(iz * 16 + h * 8, 8)
                    p = slots[slot, 0, row, at, :]
                    g = p + cx * minmod(
                        slots[slot, 2, row, at, :] - p, p - slots[slot, 1, row, at, :]
                    )
                    gx[r, at, :] = g
                    v[h][iz] = g
            q, _w = quads(v[0], v[1], y)
            for k in range(4):
                parts[2 * k + row] = q[k]
        sx[o] = stack_sums(parts, sub)

    half_step(0, 0)
    arrival(0, near(1), a1)
    rolls(0)
    half_step(1, 1)

    @pl.loop(1, 8)
    def _(k):
        i = 2 * k
        arrival(0, near(i), a1)
        rolls(1)
        half_step(i, 0)
        x_faces(i - 2, 0)
        arrival(0, near(i + 1), a1)
        rolls(0)
        half_step(i + 1, 1)
        x_faces(i - 1, 1)

    rolls(1)
    x_faces(14, 0)
    x_faces(15, 1)

    for ghost, real in ((1, 2), (0, 3), (34, 33), (35, 32)):
        for iz in range(8):
            lo, hi = pl.ds(iz * 16, 8), pl.ds(iz * 16 + 8, 8)
            x0, x1 = plus[real, lo, :], plus[real, hi, :]
            plus[ghost, lo, :] = flip8(x1, sub)
            plus[ghost, hi, :] = flip8(x0, sub)

    cy = (0.5 + 0.125 * y[0], 0.5 - 0.125 * y[1])

    def y_face(j):
        v = [[None] * 8, [None] * 8]
        for iz in range(8):
            for h in range(2):
                at = pl.ds(iz * 16 + h * 8, 8)
                if h:
                    c, b, a = plus[j + 1, at, :], plus[j, at, :], plus[j + 2, at, :]
                else:
                    c, b, a = plus[j + 2, at, :], plus[j + 3, at, :], plus[j + 1, at, :]
                g = c + cy[h] * minmod(a - c, c - b)
                gy[j, at, :] = g
                v[h][iz] = g
        return quads(v[0], v[1], y)

    @pl.loop(0, N)
    def _(i):
        d = lax.rem(far(i + 1), N)
        o = lax.rem(me + d, N)
        parts = [None] * 8
        for row in range(2):
            q, _w = y_face(2 * o + row)
            for k in range(4):
                parts[2 * k + row] = q[k]
        sy[o] = stack_sums(parts, sub)

        @pl.when(d > 0)
        def _():
            vel_copy(4, d, sy.at[o], ry.at[me]).start()

    ry[me] = sy[me]
    q, w = y_face(32)
    s32[...] = stack_sums([q[0], w[0], q[1], w[1], q[2], zero, q[3], zero], sub)
    r32[me] = s32[...]

    drain(recv.at[1], rhs)
    first, second = gas(*gather_sums(rhs), sub, False)
    sets = []
    for row in range(2):
        mix, weight, ux, uy = [spread(first[2 * i + row : 2 * i + row + 1]) for i in range(4)]
        uz, half = spread(second[row : row + 1]), spread(second[2 + row : 3 + row])
        ey = [jnp.exp(-((y[h] - uy) * (y[h] - uy)) * half) for h in range(2)]
        sets.append((mix, weight, ux - xi_x, uz, half, ey))
    v = [[None] * 8, [None] * 8]
    w = [[None] * 8, [None] * 8]
    at_one = (lane & 3) == 1
    for iz in range(8):
        b = []
        for mix, weight, dx, uz, half, ey in sets:
            dz = (iz - 3.5) - uz
            b.append(weight * jnp.exp(-(dz * dz + dx * dx) * half))
        for h in range(2):
            i = iz * 2 + h
            u = sets[0][0] * hf[i] + sets[0][5][h] * b[0]
            p = sets[1][0] * pk[i] + sets[1][5][h] * b[1]
            ul, pl_ = pltpu.roll(u, 1, 1), pltpu.roll(p, 1, 1)
            ur, pr = pltpu.roll(u, 127, 1), pltpu.roll(p, 127, 1)
            inner = p + cx * minmod(
                jnp.where(at_one, ur, pr) - p, p - jnp.where(at_one, pl_, ul)
            )
            outer = u + cx * minmod(
                jnp.where(at_one, pr, ur) - u, u - jnp.where(at_one, ul, pl_)
            )
            ge[i] = inner
            gh[i] = outer
            v[h][iz] = inner
            w[h][iz] = outer

    def packed_tile(v):
        q, _w = quads(v[0], v[1], y)
        parts = [None] * 8
        for k in range(4):
            parts[2 * k] = q[k]
            parts[2 * k + 1] = pltpu.roll(q[k], 124, 1)
        return stack_sums(parts, sub)

    inner, outer = packed_tile(v), packed_tile(w)
    sex[...] = jnp.where(is_pos, inner, pltpu.roll(outer, 127, 1))
    edges = jnp.where(is_pos & ((lane & 7) == 1), outer, inner)

    @pl.loop(0, N)
    def _(i):
        d = lax.rem(far(i + 1), N)
        o = lax.rem(me + d, N)
        sx[o] = jnp.where(
            at_edge, pltpu.roll(edges, 126 - 8 * o + ip, 1), pltpu.roll(sx[o], ip, 1)
        )

        @pl.when(d > 0)
        def _():
            vel_copy(3, d, sx.at[o], rx.at[me]).start()

    rx[me] = sx[me]
    rex[me] = sex[...]

    @pl.loop(1, N)
    def _(i):
        d = far(i)
        vel_copy(5, d, s32, r32.at[me]).start()
        vel_copy(6, d, sex, rex.at[me]).start()

    @pl.loop(0, N)
    def _(o):
        for i in range(16):
            at = pl.ds(i * 8, 8)
            e = jnp.where(is_pos & at_one, gh[i], ge[i])
            for row in range(2):
                r = 2 * o + row
                gx[r, at, :] = jnp.where(
                    at_edge,
                    pltpu.roll(e, 126 - 4 * r + ip, 1),
                    pltpu.roll(gx[r, at, :], ip, 1),
                )

    @pl.loop(0, ROWS)
    def _(r):
        for i in range(16):
            at = pl.ds(i * 8, 8)
            fv[r, at, :] = (4.0 / 3.0) * plus[r + 2, at, :] - fv[r, at, :] * (1.0 / 3.0)

    drain(hrecv.at[0], warm)
    label = spread(lab_ref[...])
    walled = label >= 0
    by_lane = lax.broadcasted_iota(jnp.int32, (16, LANES), 1)
    by_row = lax.broadcasted_iota(jnp.int32, (16, LANES), 0)
    on_diag = by_lane == by_row

    def column(k):
        return jnp.sum(
            jnp.where(on_diag, jnp.broadcast_to(warm[k], (16, LANES)), 0.0),
            axis=1, keepdims=True,
        )

    tw_sum = jnp.zeros((16, LANES), F32)
    label16 = jnp.broadcast_to(lab_ref[...], (16, LANES))
    for k in range(N):
        tw_sum = tw_sum + jnp.where(label16 == k * 16 + by_row, column(k), 0.0)
    tw_sum = tw_sum[0:8] + tw_sum[8:16]
    tw = jnp.where(walled, spread(jnp.sum(tw_sum, axis=0, keepdims=True)), 1.0)
    half_tw = 0.5 / tw
    wall_norm = jnp.exp(-1.5 * jnp.log(TWO_PI * tw))
    e_xy = jnp.exp(-(y[1] * y[1]) * half_tw)
    e_z = jnp.exp(-(zed * zed) * half_tw)

    def down(t):
        return spread(jnp.sum(t, axis=0, keepdims=True))

    sum_x, sum_xx = 2.0 * down(e_xy), 2.0 * down(y[1] * y[1] * e_xy)
    sum_z, sum_zz = down(e_z), down(zed * zed * e_z)
    sum_y1, sum_y3 = down(y[1] * e_xy), down(y[1] * y[1] * y[1] * e_xy)
    out_mass = wall_norm * (sum_x * sum_z * sum_y1)
    out_energy = 0.5 * wall_norm * (
        sum_xx * sum_z * sum_y1 + sum_x * sum_zz * sum_y1 + sum_x * sum_z * sum_y3
    )

    drain(send.at[1], rhs)
    drain(send.at[2], a1)
    to_right.wait_send()
    to_left.wait_send()

    drain(recv.at[4], ry)
    first, second = gas(*gather_sums(ry), sub, True)
    ay[me, 0:8, :] = first
    ay[me, 8:12, :] = second[0:4]

    @pl.loop(1, N)
    def _(i):
        vel_copy(8, far(i), ay.at[me], ay.at[me], 1).start()

    drain(recv.at[3], rx)
    first, second = gas(*gather_sums(rx), sub, True)
    ax[me, 0:8, :] = first
    ax[me, 8:12, :] = second[0:4]

    @pl.loop(1, N)
    def _(i):
        vel_copy(7, far(i), ax.at[me], ax.at[me], 2).start()

    drain(recv.at[5], r32)
    total, by_x, by_xx = gather_sums(r32)
    wall_first, wall_second = gas(total, by_x, by_xx, sub, True)
    in_mass = spread(total[1:2])
    in_energy = 0.5 * spread(by_xx[1:2] + total[3:4])
    rho_w = in_mass / out_mass
    flow = jnp.where(walled, 0.25 * (in_energy - rho_w * out_energy), 0.0)
    heat[sp] = jnp.where(sub == 0, flow, label.astype(F32))

    @pl.loop(1, N)
    def _(d):
        space_copy(1, d, heat.at[sp], heat.at[sp]).start()

    flux = y_flux(wall_first, wall_second, 0, gy, 32, xi_x)
    ey_w = jnp.exp(-(y[0] * y[0]) * half_tw) * (0.25 * y[0])
    bz_w = rho_w * wall_norm * jnp.exp(-(zed * zed + xi_x * xi_x) * half_tw)
    for iz in range(8):
        b = spread(bz_w[iz : iz + 1])
        wf[2 * iz] = jnp.where(walled, ey_w * b, flux[2 * iz])
        wf[2 * iz + 1] = jnp.where(
            walled, (0.25 * y[1]) * gy[32, pl.ds(iz * 16 + 8, 8), :], flux[2 * iz + 1]
        )

    drain(recv.at[6], rex)
    first, second = gas(*gather_sums(rex), sub, True)
    first, second = pltpu.roll(first, 1 - ip, 1), pltpu.roll(second, 1 - ip, 1)
    even = (lane & 7) == 2 - ip

    def packed(t, i):
        return jnp.where(even, spread(t[i : i + 1]), pltpu.roll(spread(t[i + 1 : i + 2]), 4, 1))

    quarter_x = 0.25 * xi_x
    mix, weight, ux, uy = [packed(first, 2 * i) for i in range(4)]
    uz, half = packed(second, 0), packed(second, 2)
    ey = [jnp.exp(-((y[h] - uy) * (y[h] - uy)) * half) for h in range(2)]
    dx = xi_x - ux
    for iz in range(8):
        dz = (iz - 3.5) - uz
        b = quarter_x * weight * jnp.exp(-(dz * dz + dx * dx) * half)
        for h in range(2):
            i = iz * 2 + h
            g = jnp.where(is_pos, ge[i], gh[i])
            hf[i] = (quarter_x * mix) * g + ey[h] * b

    last = lane == 127

    @pl.loop(0, N)
    def _(o):
        for i in range(16):
            at = pl.ds(i * 8, 8)
            for row in range(2):
                r = 2 * o + row
                fv[r, at, :] = fv[r, at, :] - jnp.where(
                    last, pltpu.roll(hf[i], 125 - 4 * r + ip, 1), 0.0
                )

    for i in range(16):
        at = pl.ds(i * 8, 8)
        fv[31, at, :] = fv[31, at, :] - wf[i]
    drain(send.at[3], rx)
    drain(send.at[4], ry)
    drain(send.at[5], r32)
    drain(send.at[6], rex)
    drain(hsend.at[0], warm)

    def y_update(i):
        o = owner(i)
        first, second = ay[o, 0:8, :], ay[o, 8:12, :]
        low = y_flux(first, second, 0, gy, 2 * o, xi_x)
        high = y_flux(first, second, 1, gy, 2 * o + 1, xi_x)
        rows = (above(2 * o), 2 * o, 2 * o + 1)
        for k in range(0, 16, 8):
            ats = [pl.ds(i * 8, 8) for i in range(k, k + 8)]
            old = [[fv[r, at, :] for at in ats] for r in rows]
            for i, at in enumerate(ats):
                fv[rows[0], at, :] = old[0][i] - low[k + i]
                fv[rows[1], at, :] = old[1][i] + (low[k + i] - high[k + i])
                fv[rows[2], at, :] = old[2][i] + high[k + i]

    def above(r):
        return jnp.where(r == 0, ROWS, r - 1)

    y_update(0)

    @pl.loop(1, N)
    def _(i):
        arrival(1, near(i), ay)
        y_update(i)

    def x_flux(i, slot):
        o = owner(i)
        first, second = ax[o, 0:8, :], ax[o, 8:12, :]
        for row in range(2):
            mix, ey, bz = factors(first, second, row, y, zed, xi_x)
            mix = quarter_x * mix
            bz = quarter_x * bz
            for iz in range(8):
                b = spread(bz[iz : iz + 1])
                for h in range(2):
                    at = pl.ds(iz * 16 + h * 8, 8)
                    fresh[slot, row, at, :] = mix * gx[2 * o + row, at, :] + ey[h] * b

    def x_rolls(slot):
        for row in range(2):
            for k in range(16):
                at = pl.ds(k * 8, 8)
                flux = fresh[slot, row, at, :]
                slots[slot, 0, row, at, :] = flux
                slots[slot, 1, row, at, :] = pltpu.roll(flux, 127, 1)

    def x_update(i, slot):
        o = owner(i)
        for row in range(2):
            r = 2 * o + row
            for k in range(16):
                at = pl.ds(k * 8, 8)
                beyond = jnp.where(last, 0.0, slots[slot, 1, row, at, :])
                plus[r, at, :] = fv[r, at, :] + (slots[slot, 0, row, at, :] - beyond)
            pltpu.make_async_copy(plus.at[r], out_hbm.at[:, r], out_sem.at[r]).start()

    x_flux(0, 0)
    arrival(2, near(1), ax)
    x_rolls(0)
    x_flux(1, 1)

    @pl.loop(1, 8)
    def _(k):
        i = 2 * k
        arrival(2, near(i), ax)
        x_rolls(1)
        x_flux(i, 0)
        x_update(i - 2, 0)
        arrival(2, near(i + 1), ax)
        x_rolls(0)
        x_flux(i + 1, 1)
        x_update(i - 1, 1)

    x_rolls(1)
    x_update(14, 0)
    x_update(15, 1)

    drain(hrecv.at[1], heat)
    piece = lax.broadcasted_iota(jnp.int32, (16, LANES), 0) + sp * 16
    piecef = piece.astype(F32)
    gained = jnp.zeros((16, LANES), F32)
    for k in range(N):
        t = heat[k]
        gained = gained + jnp.where(
            jnp.broadcast_to(t[1:2], (16, LANES)) == piecef,
            jnp.broadcast_to(t[0:1], (16, LANES)),
            0.0,
        )
    gained = jnp.sum(gained, axis=1, keepdims=True)
    own = jnp.broadcast_to(column(sp), (16, LANES))
    dev = own - 1.0
    before = column(lax.rem(sp + N - 1, N))[15:16] - 1.0
    after = column(lax.rem(sp + 1, N))[0:1] - 1.0
    before = jnp.broadcast_to(jnp.where(sp == 0, 0.0, 1.0) * before, (1, LANES))
    after = jnp.broadcast_to(jnp.where(sp == N - 1, 0.0, 1.0) * after, (1, LANES))
    dev_before = jnp.concatenate([before, dev[:-1]], axis=0)
    dev_after = jnp.concatenate([dev[1:], after], axis=0)
    new = own + 0.45 * (dev_before - 2.0 * dev + dev_after) + 0.025 * gained
    rev_ref[...] = jnp.sum(jnp.where(on_diag, new, 0.0), axis=0, keepdims=True)[:, 0:16]

    rev_copy = pltpu.make_async_copy(rev_ref, rev_hbm, out_sem.at[ROWS])
    rev_copy.start()
    drain(send.at[7], ax)
    drain(hsend.at[1], heat)

    drain(send.at[8], ay)
    rev_copy.wait()

    @pl.loop(0, ROWS)
    def _(r):
        pltpu.make_async_copy(plus.at[r], out_hbm.at[:, r], out_sem.at[r]).wait()


def hand_over(from_hbm, rev_from, to_hbm, rev_to, held, rev_held, sem):
    pieces = [(from_hbm.at[pl.ds(16 * i, 16)], held.at[i], to_hbm.at[pl.ds(16 * i, 16)]) for i in range(8)]
    pieces.append((rev_from, rev_held, rev_to))
    copies = [
        (pltpu.make_async_copy(a, b, sem.at[0, i]), pltpu.make_async_copy(b, c, sem.at[1, i]))
        for i, (a, b, c) in enumerate(pieces)
    ]
    for c, _d in copies:
        c.start()
    for c, d in copies:
        c.wait()
        d.start()
    for _c, d in copies:
        d.wait()


def per_device(particle_distribution, piece_warmth, exterior_piece_label):
    tile = functools.partial(pltpu.VMEM, dtype=F32)
    dma = pltpu.SemaphoreType.DMA
    hbm = pl.BlockSpec(memory_space=pltpu.HBM)
    one = tile((N, 8, LANES))
    two = tile((N, 12, LANES))
    flat = tile((8, LANES))
    shape = functools.partial(jax.ShapeDtypeStruct, dtype=F32)
    out, revised = pl.pallas_call(
        kernel,
        out_shape=(shape(particle_distribution.shape), shape((1, 16))),
        in_specs=[hbm] * 3,
        out_specs=(hbm, hbm),
        scratch_shapes=[
            tile((ROWS + 1, 128, LANES)), tile((ROWS + 1, 128, LANES)), two, one, tile((1, 16)),
            tile((ROWS + 4, 128, LANES)), tile((ROWS, 128, LANES)),
            tile((1, 16)), pltpu.VMEM((1, LANES), jnp.int32),
            one, one, two,
            one, one, two,
            one, one,
            flat, one,
            flat, one,
            flat, one,
            tile((N, 1, LANES)), one,
            one, one, one, one, one, one, tile((2, 3, 2, 128, LANES)), tile((2, 2, 128, LANES)),
            dma((ROWS + 2,)), dma((ROWS + 1,)),
            dma((9,)), dma((9,)), dma((3, N)), dma((4,)), dma((4,)),
        ],
        compiler_params=pltpu.CompilerParams(
            collective_id=0, has_side_effects=True, vmem_limit_bytes=62 * 1024 * 1000
        ),
    )(
        particle_distribution,
        piece_warmth.reshape(1, 16),
        exterior_piece_label.reshape(1, LANES),
    )
    out, revised = pl.pallas_call(
        hand_over,
        out_shape=(shape(particle_distribution.shape), shape((1, 16))),
        in_specs=[hbm] * 2,
        out_specs=(hbm, hbm),
        scratch_shapes=[tile((8, 16, ROWS, LANES)), tile((1, 16)), dma((2, 9))],
        compiler_params=pltpu.CompilerParams(vmem_limit_bytes=62 * 1024 * 1000),
    )(out, revised)
    return out, revised.reshape(16)


def solution(mesh):
    return jax.shard_map(
        per_device,
        mesh=mesh,
        in_specs=(P("vel", None, "space"), P("space"), P("space")),
        out_specs=(P("vel", None, "space"), P("space")),
        check_vma=False,
    )
```

time: 49.2 us -> 42.8 us (0.87)
  local copies, waits for them, and re-layouts: 3.6 us -> 0 us
  Pallas kernels: 44.8 us -> 42 us
    pallas_call x1, Pallas kernels: 44.8 us -> 39.6 us  [per_device(): pl.pallas_call(kernel, out_shape=(shape(particle_distribution.shape), sha...]
    unnamed x4 -> x0, local copies, waits for them, and re-layouts: 3.6 us -> none
    pallas_call x0 -> x1, Pallas kernels: none -> 2.42 us  [per_device(): pl.pallas_call(hand_over, out_shape=(shape(particle_distribution.shape),...]
where the time goes in v3:
time: 42.8 us; the launch traced here: 42.6 us
  Pallas kernels  42 us (98%)
  between operations  0.64 us (1%)
    pallas_call x1, Pallas kernels, per_device(): pl.pallas_call(kernel, out_shape=(shape(particle_distribution.shape), sha...  39.6 us
    pallas_call x1, Pallas kernels, per_device(): pl.pallas_call(hand_over, out_shape=(shape(particle_distribution.shape),...  2.42 us

profile of v3, /device:TPU:1, one launch (start us, length us, event | category | flops | bytes accessed | tf_op | source)
XLA Modules:
  0.0 42.6 jit_solution(2454172032632945713)
XLA Ops:
  0.6 39.6 %shard_map.50 = (f32[128,32,128]{2,1,0:T(8,128)}, f32[1,16]{1,0:T(1,128)}) custom-call(f32[128,32,128]{2,1,0:T(8,128)} %f_hbm.1, f32[1,16]{1,0:T(1,128)} %bitcast.3, s32[1,128]{1,0:T(1,128)} %bitcast.4), custom_call_target="tpu_custom_call" | custom-call | tf_op jit(solution)/shard_map/pallas_call | solution.py:752
  40.2 2.4 %shard_map.51 = (f32[128,32,128]{2,1,0:T(8,128)}, f32[1,16]{1,0:T(1,128)}) custom-call(f32[128,32,128]{2,1,0:T(8,128)} %get-tuple-element.6.from_hbm, f32[1,16]{1,0:T(1,128)} %get-tuple-element.7.rev_from), custom_call_target="tpu_custom_call" | custom-call | tf_op jit(solution)/shard_map/pallas_call | solution.py:780
